TPU v7x, 256 devices: a whole 4x4x8 slice. The times are simulated.
256 devices in a mesh: row: 16 (over z_hi, y), col: 16 (over x, z_lo, core).
Axes of the slice: x: 4, y: 4, z: 8 (z_hi: 4, z_lo: 2; z = z_hi * 2 + z_lo), core: 2. Of those that a mesh axis runs over, the one named last changes fastest.
Arguments:
- object_field: float32 [2, 8192, 8192], P(None, 'row', 'col'), may hold values from -6 to 6
- probe: float32 [2, 2, 256, 256], replicated, may hold values from -6 to 6
- own_pos: int32 [1024, 2], P(('row', 'col')), may hold values from 0 to 7936, as said below
- own_amp: bfloat16 [1024, 256, 256], P(('row', 'col')), may hold values from 0 to 4
- lend_pos: int32 [512, 2], P(('row', 'col')), may hold values from 0 to 7936, as said below
- lend_live: int32 [512], P(('row', 'col')), may hold values from 0 to 1, as said below
- recv_amp: bfloat16 [512, 256, 256], P(('row', 'col')), may hold values from 0 to 4
Outputs:
- new_object: float32 [2, 8192, 8192], P(None, 'row', 'col')
- probe_grad: float32 [2, 2, 256, 256], replicated
Inputs may be any that keep to these rules, and one draw needn't show every extreme that they name: `own_pos`: each frame of tile (i, j) lies inside the object and its offset is at most 128 before the tile's first pixel and at most 384 after it, along both dimensions. `lend_pos`: offsets as for own_pos, relative to the lending tile, also where the slot is empty. `lend_live`: slots to the next column are 0 in the last tile column, slots to the previous column are 0 in the first.
All inputs are finite; a program needn't handle non-finite values.
Results may differ from a plain program's by a relative error of at most 0.00045.
Values may be sent and summed in bfloat16 or wider, within the bound.
A program may use at most 128 MiB of HBM per device.

v0:
```python
import math

import jax
import jax.numpy as jnp
from jax import lax
from jax.sharding import PartitionSpec as P

highest_precision = lax.Precision.HIGHEST


def with_halo(array, sides, width):
    for axis, dim in sides:
        peers, length = (lax.axis_size(axis), array.shape[dim])
        up = [(i, (i + 1) % peers) for i in range(peers - 1)]
        down = [(j, i) for i, j in up]
        last = lax.slice_in_dim(array, length - width, length, axis=dim)
        initial = lax.slice_in_dim(array, 0, width, axis=dim)
        before = lax.ppermute(last, axis, up)
        after = lax.ppermute(initial, axis, down)
        array = jnp.concatenate([before, array, after], axis=dim)
    return array


def passed_along(value, axis, steps):
    count = lax.axis_size(axis)
    initial, last = (max(0, -steps), min(count, count - steps))
    return lax.ppermute(value, axis, [(source, source + steps) for source in range(initial, last)])


def dft_tables(length):
    counter = jnp.arange(length, dtype=jnp.int32)
    product = counter[:, None] * counter[None, :] % length
    angles = product.astype(jnp.float32) * (2.0 * math.pi / length)
    scaling = 1.0 / math.sqrt(length)
    return (jnp.cos(angles) * scaling, jnp.sin(angles) * scaling)


def left_product(table, values):
    return jnp.einsum("kn,...nm->...km", table, values, precision=highest_precision)


def right_product(values, table):
    return jnp.einsum("...kn,nm->...km", values, table, precision=highest_precision)


def transform(real_part, imag_part, cosine, sine, direction):
    left_real = left_product(cosine, real_part) - direction * left_product(sine, imag_part)
    left_imag = left_product(cosine, imag_part) + direction * left_product(sine, real_part)
    out_real = right_product(left_real, cosine) - direction * right_product(left_imag, sine)
    out_imag = right_product(left_imag, cosine) + direction * right_product(left_real, sine)
    return (out_real, out_imag)


def frame_terms(patches, amplitudes, probe, cosine, sine):
    probe_real = probe[:, 0][None]
    probe_imag = probe[:, 1][None]
    patch_real = patches[:, 0][:, None]
    patch_imag = patches[:, 1][:, None]
    exit_real = probe_real * patch_real - probe_imag * patch_imag
    exit_imag = probe_real * patch_imag + probe_imag * patch_real
    far_real, far_imag = transform(exit_real, exit_imag, cosine, sine, -1.0)
    power = jnp.sum(far_real * far_real + far_imag * far_imag, axis=1)
    ratio = amplitudes.astype(jnp.float32) / jnp.maximum(jnp.sqrt(power), 1.0)
    keeping = (1.0 - ratio)[:, None]
    back_real, back_imag = transform(far_real * keeping, far_imag * keeping, cosine, sine, 1.0)
    object_real = jnp.sum(probe_real * back_real + probe_imag * back_imag, axis=1)
    object_imag = jnp.sum(probe_real * back_imag - probe_imag * back_real, axis=1)
    grad_real = jnp.sum(patch_real * back_real + patch_imag * back_imag, axis=0)
    grad_imag = jnp.sum(patch_real * back_imag - patch_imag * back_real, axis=0)
    return (
        jnp.stack([object_real, object_imag], axis=1),
        jnp.stack([grad_real, grad_imag], axis=1),
    )


def shards(object_field, probe, own_pos, own_amp, lend_pos, lend_live, recv_amp):
    frame_len = probe.shape[-1]
    half_width = frame_len // 2
    tile_len = object_field.shape[1]
    own_count = own_pos.shape[0]
    lend_count = lend_pos.shape[0] // 2
    cosine, sine = dft_tables(frame_len)
    row_anchor = lax.axis_index("row") * tile_len - half_width
    col_anchor = lax.axis_index("col") * tile_len - half_width
    zero_start = jnp.zeros((), jnp.int32)
    widened = with_halo(object_field, (("row", 1), ("col", 2)), half_width)

    def local_offsets(positions):
        return (positions[:, 0] - row_anchor, positions[:, 1] - col_anchor)

    def cut_patches(positions):
        rows_at, cols_at = local_offsets(positions)

        def single(row_start, col_start):
            return lax.dynamic_slice(
                widened, (zero_start, row_start, col_start), (2, frame_len, frame_len)
            )

        return jax.vmap(single)(rows_at, cols_at)

    own_patches = cut_patches(own_pos)
    lent_patches = cut_patches(lend_pos) * lend_live.astype(jnp.float32)[:, None, None, None]

    def pass_patches(shard_block, offset):
        return passed_along(shard_block, "col", offset)

    received = jnp.concatenate(
        [pass_patches(lent_patches[:lend_count], 1), pass_patches(lent_patches[lend_count:], -1)],
        axis=0,
    )
    object_terms, probe_parts = frame_terms(
        jnp.concatenate([own_patches, received], axis=0),
        jnp.concatenate([own_amp, recv_amp], axis=0),
        probe,
        cosine,
        sine,
    )

    def return_terms(shard_block, offset):
        return passed_along(shard_block.astype(jnp.bfloat16), "col", offset).astype(
            shard_block.dtype
        )

    remote_terms = object_terms[own_count:]
    lent_terms = jnp.concatenate(
        [return_terms(remote_terms[:lend_count], -1), return_terms(remote_terms[lend_count:], 1)],
        axis=0,
    )
    own_terms = object_terms[:own_count]
    all_terms = jnp.concatenate([own_terms, lent_terms], axis=0)
    rows_at, cols_at = local_offsets(jnp.concatenate([own_pos, lend_pos], axis=0))
    gradient = jnp.zeros_like(widened)
    for slot_index in range(all_terms.shape[0]):
        corner_start = (zero_start, rows_at[slot_index], cols_at[slot_index])
        current = lax.dynamic_slice(gradient, corner_start, (2, frame_len, frame_len))
        gradient = lax.dynamic_update_slice(gradient, current + all_terms[slot_index], corner_start)

    def pass_rows(strip, offset):
        return passed_along(strip, "row", offset)

    core_rows = gradient[:, half_width : half_width + tile_len]
    from_below = pass_rows(gradient[:, :half_width], -1)
    from_above = pass_rows(gradient[:, half_width + tile_len :], 1)
    core_rows = core_rows.at[:, tile_len - half_width :].add(from_below)
    core_rows = core_rows.at[:, :half_width].add(from_above)

    def pass_cols(strip, offset):
        return passed_along(strip.astype(jnp.bfloat16), "col", offset).astype(strip.dtype)

    inner_block = core_rows[:, :, half_width : half_width + tile_len]
    from_right = pass_cols(core_rows[:, :, :half_width], -1)
    from_left = pass_cols(core_rows[:, :, half_width + tile_len :], 1)
    inner_block = inner_block.at[:, :, tile_len - half_width :].add(from_right)
    inner_block = inner_block.at[:, :, :half_width].add(from_left)
    peak = jnp.max(jnp.sum(probe * probe, axis=(0, 1))) + 1e-06
    new_object = object_field - inner_block / peak
    summed_terms = lax.psum(probe_parts, ("row", "col"))
    probe_grad = summed_terms / (own_count * lax.axis_size("row") * lax.axis_size("col"))
    return (new_object, probe_grad)


def solution(mesh):
    placed = (
        P(None, "row", "col"),
        P(),
        P(("row", "col"), None),
        P(("row", "col"), None, None),
        P(("row", "col"), None),
        P(("row", "col")),
        P(("row", "col"), None, None),
    )
    return jax.shard_map(
        shards, mesh=mesh, in_specs=placed, out_specs=(P(None, "row", "col"), P()), check_vma=False
    )
```

profile of v0, /device:TPU:1, one launch (start us, length us, event | category | flops | bytes accessed | tf_op | source)
XLA Modules:
  0.0 576.0 jit_solution(13634489859929747364)
XLA Ops:
  9.6 4.8 collective-permute-start
  18.9 5.7 collective-permute-done
  33.1 5.3 collective-permute-start.2
  64.0 5.2 pad_maximum_fusion.1
  69.2 6.6 %while.7 = (s32[]{:T(128)}, f32[2,768,768]{2,1,0:T(8,128)}, s32[2,3]{1,0:T(2,128)S(1)}, f32[2,2,256,256]{3,2,1,0:T(8,128)S(1)}, s32[]{:T(128)}) while((s32[]{:T(128)}, f32[2,768,768]{2,1,0:T(8,128)}, s32[2,3]{1,0:T(2,128)S(1)}, f32[2,2,256,256]{3,2,1,0:T(8,128)S(1)}, s32[]{:T(128)}) %tuple.89), condition=%wide.while_cond.5, body=%wide.while_body.5.sunk | while | flops 2 | bytes 1048693 | solution.py:95
  76.1 3.6 collective-permute-start.4
  81.7 16.9 %while.6 = (s32[]{:T(128)}, f32[2,768,768]{2,1,0:T(8,128)}, s32[4,3]{1,0:T(4,128)S(1)}, f32[4,2,256,256]{3,2,1,0:T(8,128)}, s32[]{:T(128)}) while((s32[]{:T(128)}, f32[2,768,768]{2,1,0:T(8,128)}, s32[4,3]{1,0:T(4,128)S(1)}, f32[4,2,256,256]{3,2,1,0:T(8,128)}, s32[]{:T(128)}) %tuple.94), condition=%wide.while_cond.4, body=%wide.while_body.4.sunk | while | flops 2 | bytes 1050217 | solution.py:95
  100.7 6.2 %fusion.18 = f32[6,2,256,256]{3,2,1,0:T(8,128)S(1)} fusion(f32[6,256,256]{2,1,0:T(8,128)S(1)} %get-tuple-element.95, f32[2,256,256]{2,1,0:T(8,128)S(1)} %get-tuple-element.105, f32[6,256,256]{2,1,0:T(8,128)S(1)} %get-tuple-element.94, f32[2,256,256]{2,1,0:T(8,128)S(1)} %get-tuple-element.104), kind=kOutput, calls=%fused_computation.42 | convolution fusion | flops 2419261440 | bytes 7340032 | tf_op jit(solution)/shard_map/kn,...nm->...km/dot_general | solution.py:39
  106.9 6.6 %fusion.19 = f32[6,2,256,256]{3,2,1,0:T(8,128)S(1)} fusion(f32[6,256,256]{2,1,0:T(8,128)S(1)} %get-tuple-element.95, f32[2,256,256]{2,1,0:T(8,128)S(1)} %get-tuple-element.105, f32[6,256,256]{2,1,0:T(8,128)S(1)} %get-tuple-element.94, f32[2,256,256]{2,1,0:T(8,128)S(1)} %get-tuple-element.104), kind=kOutput, calls=%fused_computation.44 | convolution fusion | flops 2419261440 | bytes 7340032 | tf_op jit(solution)/shard_map/kn,...nm->...km/dot_general | solution.py:39
  113.5 6.5 %multiply_add_fusion.1 = f32[6,2,256,256]{3,2,1,0:T(8,128)S(1)} fusion(f32[6,2,256,256]{3,2,1,0:T(8,128)S(1)} %fusion.19, f32[6,256,256]{2,1,0:T(8,128)S(1)} %get-tuple-element.95, f32[2,256,256]{2,1,0:T(8,128)S(1)} %get-tuple-element.105, f32[6,256,256]{2,1,0:T(8,128)S(1)} %get-tuple-element.94, f32[2,256,256]{2,1,0:T(8,128)S(1)} %get-tuple-element.104), kind=kOutput, calls=%fused_computation.38 | convolution fusion | flops 2420834304 | bytes 10485760 | tf_op jit(solution)/shard_map/kn,...nm->...km/dot_general | solution.py:39
  120.0 6.7 %fusion.11 = f32[6,2,256,256]{3,2,1,0:T(8,128)S(1)} fusion(f32[6,2,256,256]{3,2,1,0:T(8,128)S(1)} %multiply_add_fusion.1), kind=kOutput, calls=%fused_computation.25 | convolution fusion | flops 2416902144 | bytes 6291456 | tf_op jit(solution)/shard_map/...kn,nm->...km/dot_general | solution.py:43
  126.7 6.2 %fusion.9 = f32[6,2,256,256]{3,2,1,0:T(8,128)S(1)} fusion(f32[6,2,256,256]{3,2,1,0:T(8,128)S(1)} %multiply_add_fusion.1), kind=kOutput, calls=%fused_computation.23 | convolution fusion | flops 2416902144 | bytes 6291456 | tf_op jit(solution)/shard_map/...kn,nm->...km/dot_general | solution.py:43
  133.0 6.9 %multiply_subtract_fusion.1 = f32[6,2,256,256]{3,2,1,0:T(8,128)S(1)} fusion(f32[6,2,256,256]{3,2,1,0:T(8,128)S(1)} %fusion.18, f32[6,256,256]{2,1,0:T(8,128)S(1)} %get-tuple-element.95, f32[2,256,256]{2,1,0:T(8,128)S(1)} %get-tuple-element.105, f32[6,256,256]{2,1,0:T(8,128)S(1)} %get-tuple-element.94, f32[2,256,256]{2,1,0:T(8,128)S(1)} %get-tuple-element.104), kind=kOutput, calls=%fused_computation.39 | convolution fusion | flops 2420834304 | bytes 10485760 | tf_op jit(solution)/shard_map/kn,...nm->...km/dot_general | solution.py:39
  139.9 6.6 %multiply_subtract_fusion = f32[6,2,256,256]{3,2,1,0:T(8,128)S(1)} fusion(f32[6,2,256,256]{3,2,1,0:T(8,128)S(1)} %fusion.11, f32[6,2,256,256]{3,2,1,0:T(8,128)S(1)} %multiply_subtract_fusion.1), kind=kOutput, calls=%fused_computation.37 | convolution fusion | flops 2418475008 | bytes 9437184 | tf_op jit(solution)/shard_map/...kn,nm->...km/dot_general | solution.py:43
  146.5 7.2 %add_reduce_fusion.2 = (f32[6,256,256]{2,1,0:T(8,128)S(1)}, f32[6,2,256,256]{3,2,1,0:T(8,128)S(1)}) fusion(f32[6,2,256,256]{3,2,1,0:T(8,128)S(1)} %multiply_subtract_fusion, f32[6,2,256,256]{3,2,1,0:T(8,128)S(1)} %fusion.9, f32[6,2,256,256]{3,2,1,0:T(8,128)S(1)} %multiply_subtract_fusion.1), kind=kOutput, calls=%fused_computation.35 | convolution fusion | flops 2421227520 | bytes 14155776 | tf_op jit(solution)/shard_map/...kn,nm->...km/dot_general | solution.py:43
  154.3 6.2 %fusion.23 = f32[6,2,256,256]{3,2,1,0:T(8,128)S(1)} fusion(f32[6,2,256,256]{3,2,1,0:T(8,128)S(1)} %get-tuple-element.127, f32[6,256,256]{2,1,0:T(8,128)S(1)} %divide_subtract_fusion.1), kind=kOutput, calls=%fused_computation.48 | convolution fusion | flops 2417688576 | bytes 7864320 | tf_op jit(solution)/shard_map/kn,...nm->...km/dot_general | solution.py:39
  160.5 6.4 %fusion.21 = f32[6,2,256,256]{3,2,1,0:T(8,128)S(1)} fusion(f32[6,2,256,256]{3,2,1,0:T(8,128)S(1)} %get-tuple-element.127, f32[6,256,256]{2,1,0:T(8,128)S(1)} %divide_subtract_fusion.1), kind=kOutput, calls=%fused_computation.46 | convolution fusion | flops 2417688576 | bytes 7864320 | tf_op jit(solution)/shard_map/kn,...nm->...km/dot_general | solution.py:39
  167.0 6.3 %fusion.32 = f32[6,2,256,256]{3,2,1,0:T(8,128)S(1)} fusion(f32[6,2,256,256]{3,2,1,0:T(8,128)S(1)} %fusion.21, f32[6,2,256,256]{3,2,1,0:T(8,128)S(1)} %multiply_subtract_fusion, f32[6,256,256]{2,1,0:T(8,128)S(1)} %divide_subtract_fusion.1), kind=kOutput, calls=%fused_computation.56 | convolution fusion | flops 2418475008 | bytes 11010048 | tf_op jit(solution)/shard_map/kn,...nm->...km/dot_general | solution.py:39
  173.3 6.9 %fusion.3 = f32[6,2,256,256]{3,2,1,0:T(8,128)S(1)} fusion(f32[6,2,256,256]{3,2,1,0:T(8,128)S(1)} %fusion.32), kind=kOutput, calls=%fused_computation.17 | convolution fusion | flops 2416902144 | bytes 6291456 | tf_op jit(solution)/shard_map/...kn,nm->...km/dot_general | solution.py:43
  180.2 6.2 %fusion.1 = f32[6,2,256,256]{3,2,1,0:T(8,128)S(1)} fusion(f32[6,2,256,256]{3,2,1,0:T(8,128)S(1)} %fusion.32), kind=kOutput, calls=%fused_computation.15 | convolution fusion | flops 2416902144 | bytes 6291456 | tf_op jit(solution)/shard_map/...kn,nm->...km/dot_general | solution.py:43
  186.4 6.5 %fusion.29 = f32[6,2,256,256]{3,2,1,0:T(8,128)S(1)} fusion(f32[6,2,256,256]{3,2,1,0:T(8,128)S(1)} %fusion.23, f32[6,2,256,256]{3,2,1,0:T(8,128)S(1)} %multiply_subtract_fusion, f32[6,256,256]{2,1,0:T(8,128)S(1)} %divide_subtract_fusion.1), kind=kOutput, calls=%fused_computation.55 | convolution fusion | flops 2418475008 | bytes 11010048 | tf_op jit(solution)/shard_map/kn,...nm->...km/dot_general | solution.py:39
  192.9 6.3 %fusion.39 = f32[6,2,256,256]{3,2,1,0:T(8,128)S(1)} fusion(f32[6,2,256,256]{3,2,1,0:T(8,128)S(1)} %fusion.3, f32[6,2,256,256]{3,2,1,0:T(8,128)S(1)} %fusion.29), kind=kOutput, calls=%fused_computation.57 | convolution fusion | flops 2417688576 | bytes 9437184 | tf_op jit(solution)/shard_map/...kn,nm->...km/dot_general | solution.py:43
  199.2 9.5 %add_reduce_fusion = (f32[2,256,256]{2,1,0:T(8,128)}, f32[2,256,256]{2,1,0:T(8,128)}, f32[6,256,256]{2,1,0:T(8,128)S(1)}, f32[6,256,256]{2,1,0:T(8,128)S(1)}) fusion(f32[6,2,256,256]{3,2,1,0:T(8,128)S(1)} %fusion.39, f32[6,256,256]{2,1,0:T(8,128)S(1)} %get-tuple-element.95, f32[6,256,256]{2,1,0:T(8,128)S(1)} %get-tuple-element.94, ...), kind=kOutput, calls=%fused_computation.32 | convolution fusion | flops 2429222912 | bytes 17825792 | tf_op jit(solution)/shard_map/...kn,nm->...km/dot_general | solution.py:43
  214.8 6.7 %dynamic_update_slice.18 = f32[2,768,768]{2,1,0:T(8,128)} dynamic-update-slice(f32[2,768,768]{2,1,0:T(8,128)} %broadcast_in_dim.2, f32[2,256,256]{2,1,0:T(8,128)} %fusion.68, s32[]{:T(128)} %constant.144.clone.1, s32[]{:T(128)S(6)} %select_n.104, s32[]{:T(128)S(6)} %select_n.105) | dynamic-update-slice | bytes 1048580 | tf_op jit(solution)/shard_map/dynamic_update_slice | solution.py:136
  223.7 6.6 %dynamic_update_slice.19 = f32[2,768,768]{2,1,0:T(8,128)} dynamic-update-slice(f32[2,768,768]{2,1,0:T(8,128)} %dynamic_update_slice.18, f32[2,256,256]{2,1,0:T(8,128)} %fusion.71, s32[]{:T(128)} %constant.144.clone.1, s32[]{:T(128)S(6)} %select_n.106, s32[]{:T(128)S(6)} %select_n.107) | dynamic-update-slice | bytes 1048580 | tf_op jit(solution)/shard_map/dynamic_update_slice | solution.py:136
  232.5 6.6 %dynamic_update_slice.20 = f32[2,768,768]{2,1,0:T(8,128)} dynamic-update-slice(f32[2,768,768]{2,1,0:T(8,128)} %dynamic_update_slice.19, f32[2,256,256]{2,1,0:T(8,128)} %fusion.74, s32[]{:T(128)} %constant.144.clone.1, s32[]{:T(128)S(6)} %select_n.108, s32[]{:T(128)S(6)} %select_n.109) | dynamic-update-slice | bytes 1048580 | tf_op jit(solution)/shard_map/dynamic_update_slice | solution.py:136
  244.1 6.4 %dynamic_update_slice.21 = f32[2,768,768]{2,1,0:T(8,128)} dynamic-update-slice(f32[2,768,768]{2,1,0:T(8,128)} %dynamic_update_slice.20, f32[2,256,256]{2,1,0:T(8,128)} %fusion.77, s32[]{:T(128)} %constant.144.clone.1, s32[]{:T(128)S(6)} %select_n.110, s32[]{:T(128)S(6)} %select_n.111) | dynamic-update-slice | bytes 1048580 | tf_op jit(solution)/shard_map/dynamic_update_slice | solution.py:136
  251.9 6.8 %dynamic_update_slice.22 = f32[2,768,768]{2,1,0:T(8,128)} dynamic-update-slice(f32[2,768,768]{2,1,0:T(8,128)} %dynamic_update_slice.21, f32[2,256,256]{2,1,0:T(8,128)S(1)} %convert_add_fusion.1, s32[]{:T(128)} %constant.144.clone.1, s32[]{:T(128)S(6)} %select_n.112, s32[]{:T(128)S(6)} %select_n.113) | dynamic-update-slice | bytes 1048580 | tf_op jit(solution)/shard_map/dynamic_update_slice | solution.py:136
  260.1 6.6 %dynamic_update_slice.23 = f32[2,768,768]{2,1,0:T(8,128)} dynamic-update-slice(f32[2,768,768]{2,1,0:T(8,128)} %dynamic_update_slice.22, f32[2,256,256]{2,1,0:T(8,128)S(1)} %convert_add_fusion, s32[]{:T(128)} %constant.144.clone.1, s32[]{:T(128)S(6)} %select_n.114, s32[]{:T(128)S(6)} %select_n.115) | dynamic-update-slice | bytes 1048580 | tf_op jit(solution)/shard_map/dynamic_update_slice | solution.py:136
  270.7 5.0 collective-permute-start.9
  280.2 10.8 %collective-permute-done.8 = f32[2,128,768]{2,1,0:T(8,128)} collective-permute-done((f32[2,128,768]{2,1,0:T(8,128)}, f32[2,128,768]{2,1,0:T(8,128)}, u32[]{:S(2)}, u32[]{:S(2)}) %collective-permute-start.8) | collective-permute-done | bytes 786464 | tf_op jit(solution)/shard_map/ppermute | solution.py:27
  300.5 262.7 %all-reduce.2.cloned.1.call-done = f32[2,2,256,256]{3,2,1,0:T(8,128)} async-done(((f32[2,2,256,256]{3,2,1,0:T(8,128)}), f32[2,2,256,256]{3,2,1,0:T(8,128)}) %all-reduce.2.cloned.1.call-update) | async-done | bytes 1048592 | tf_op jit(solution)/shard_map/psum | solution.py:157
  (118 shorter events, 87.5 us)
Async XLA Ops:
  7.2 18.4 %copy-start.4 = (f32[2,512,512]{2,1,0:T(8,128)S(1)}, f32[2,512,512]{2,1,0:T(8,128)}, u32[]{:S(2)}) copy-start(f32[2,512,512]{2,1,0:T(8,128)} %param.15) | copy-start | bytes 6291460
  7.2 556.0 %all-reduce.2.cloned.1.call-start = ((), (), s32[]{:S(2)}) async-start(), calls=%async_computation | async-start | bytes 2097152 | tf_op jit(solution)/shard_map/psum | solution.py:157
  9.6 14.9 %collective-permute-start = (f32[2,128,512]{2,1,0:T(8,128)}, f32[2,128,512]{2,1,0:T(8,128)}, u32[]{:S(2)}, u32[]{:S(2)}) collective-permute-start(f32[2,128,512]{2,1,0:T(8,128)} %get-tuple-element.99), channel_id=1, source_target_pairs={{0,16},{16,32},{32,48},{48,64},{64,80},{80,96},{96,112},{112,128},... | collective-permute-start | bytes 1572872 | tf_op jit(solution)/shard_map/ppermute | solution.py:18
  14.5 14.7 %collective-permute-start.1 = (f32[2,128,512]{2,1,0:T(8,128)}, f32[2,128,512]{2,1,0:T(8,128)}, u32[]{:S(2)}, u32[]{:S(2)}) collective-permute-start(f32[2,128,512]{2,1,0:T(8,128)} %get-tuple-element.98), channel_id=1, source_target_pairs={{16,0},{32,16},{48,32},{64,48},{80,64},{96,80},{112,96},{128,112},... | collective-permute-start | bytes 1572872 | tf_op jit(solution)/shard_map/ppermute | solution.py:19
  25.8 30.4 %copy-start.13 = (s32[2]{0:T(128)S(1)}, s32[2]{0:T(128)}, u32[]{:S(2)}) copy-start(s32[2]{0:T(128)} %param.20) | copy-start | bytes 28
  25.8 38.1 %copy-start.7 = (f32[2,2,256,256]{3,2,1,0:T(8,128)S(1)}, f32[2,2,256,256]{3,2,1,0:T(8,128)}, u32[]{:S(2)}) copy-start(f32[2,2,256,256]{3,2,1,0:T(8,128)} %param.16) | copy-start | bytes 3145732
  30.2 1.6 copy-start.6
  33.1 30.9 %collective-permute-start.2 = (f32[2,768,128]{2,1,0:T(8,128)}, f32[2,768,128]{2,1,0:T(8,128)}, u32[]{:S(2)}, u32[]{:S(2)}) collective-permute-start(f32[2,768,128]{2,1,0:T(8,128)} %get-tuple-element.96), channel_id=1, source_target_pairs={{0,1},{1,2},{2,3},{3,4},{4,5},{5,6},{6,7},{7,8},{8,9},{9,10},{10,1... | collective-permute-start | bytes 2359304 | tf_op jit(solution)/shard_map/ppermute | solution.py:18
  38.4 25.7 %collective-permute-start.3 = (f32[2,768,128]{2,1,0:T(8,128)}, f32[2,768,128]{2,1,0:T(8,128)}, u32[]{:S(2)}, u32[]{:S(2)}) collective-permute-start(f32[2,768,128]{2,1,0:T(8,128)} %get-tuple-element.97), channel_id=1, source_target_pairs={{1,0},{2,1},{3,2},{4,3},{5,4},{6,5},{7,6},{8,7},{9,8},{10,9},{11,1... | collective-permute-start | bytes 2359304 | tf_op jit(solution)/shard_map/ppermute | solution.py:19
  64.0 68.9 %copy-start = (f32[2,256,256]{2,1,0:T(8,128)}, f32[2,256,256]{2,1,0:T(8,128)S(1)}, u32[]{:S(2)}) copy-start(f32[2,256,256]{2,1,0:T(8,128)S(1)} %get-tuple-element.104) | copy-start | bytes 1572868
  64.0 68.9 %copy-start.2 = (f32[2,256,256]{2,1,0:T(8,128)}, f32[2,256,256]{2,1,0:T(8,128)S(1)}, u32[]{:S(2)}) copy-start(f32[2,256,256]{2,1,0:T(8,128)S(1)} %get-tuple-element.105) | copy-start | bytes 1572868
  76.1 24.3 %collective-permute-start.4 = (f32[1,2,256,256]{3,2,1,0:T(8,128)S(1)}, f32[1,2,256,256]{3,2,1,0:T(8,128)S(1)}, u32[]{:S(2)}, u32[]{:S(2)}) collective-permute-start(f32[1,2,256,256]{3,2,1,0:T(8,128)S(1)} %get-tuple-element.107), channel_id=1, source_target_pairs={{0,1},{1,2},{2,3},{3,4},{4,5},{5,6},{6,7},{7,8},{8,9},{9,10},{10,1... | collective-permute-start | bytes 1572872 | tf_op jit(solution)/shard_map/ppermute | solution.py:27
  79.7 20.7 %collective-permute-start.5 = (f32[1,2,256,256]{3,2,1,0:T(8,128)S(1)}, f32[1,2,256,256]{3,2,1,0:T(8,128)S(1)}, u32[]{:S(2)}, u32[]{:S(2)}) collective-permute-start(f32[1,2,256,256]{3,2,1,0:T(8,128)S(1)} %get-tuple-element.106), channel_id=1, source_target_pairs={{1,0},{2,1},{3,2},{4,3},{5,4},{6,5},{7,6},{8,7},{9,8},{10,9},{11,1... | collective-permute-start | bytes 1572872 | tf_op jit(solution)/shard_map/ppermute | solution.py:27
  146.4 7.2 %copy-start.11 = (bf16[4,256,256]{2,1,0:T(8,128)(2,1)S(1)}, bf16[4,256,256]{2,1,0:T(8,128)(2,1)}, u32[]{:S(2)}) copy-start(bf16[4,256,256]{2,1,0:T(8,128)(2,1)} %param.18) | copy-start | bytes 1572868
  146.4 7.2 %copy-start.12 = (bf16[2,256,256]{2,1,0:T(8,128)(2,1)S(1)}, bf16[2,256,256]{2,1,0:T(8,128)(2,1)}, u32[]{:S(2)}) copy-start(bf16[2,256,256]{2,1,0:T(8,128)(2,1)} %param.21) | copy-start | bytes 786436
  192.8 6.3 %copy-start.1 = (f32[2,256,256]{2,1,0:T(8,128)S(1)}, f32[2,256,256]{2,1,0:T(8,128)}, u32[]{:S(2)}) copy-start(f32[2,256,256]{2,1,0:T(8,128)} %copy-done) | copy-start | bytes 1572868
  192.9 6.3 %copy-start.3 = (f32[2,256,256]{2,1,0:T(8,128)S(1)}, f32[2,256,256]{2,1,0:T(8,128)}, u32[]{:S(2)}) copy-start(f32[2,256,256]{2,1,0:T(8,128)} %copy-done.2) | copy-start | bytes 1572868
  210.5 40.0 %collective-permute-start.6 = (bf16[1,2,256,256]{3,2,1,0:T(8,128)(2,1)}, bf16[1,2,256,256]{3,2,1,0:T(8,128)(2,1)}, u32[]{:S(2)}, u32[]{:S(2)}) collective-permute-start(bf16[1,2,256,256]{3,2,1,0:T(8,128)(2,1)} %get-tuple-element.103), channel_id=1, source_target_pairs={{1,0},{2,1},{3,2},{4,3},{5,4},{6,5},{7,6},{8,7},{9,8},{10,9},{11,1... | collective-permute-start | bytes 786440 | tf_op jit(solution)/shard_map/ppermute | solution.py:27
  239.1 19.6 %collective-permute-start.7 = (bf16[1,2,256,256]{3,2,1,0:T(8,128)(2,1)S(1)}, bf16[1,2,256,256]{3,2,1,0:T(8,128)(2,1)}, u32[]{:S(2)}, u32[]{:S(2)}) collective-permute-start(bf16[1,2,256,256]{3,2,1,0:T(8,128)(2,1)S(1)} %get-tuple-element.102), channel_id=1, source_target_pairs={{0,1},{1,2},{2,3},{3,4},{4,5},{5,6},{6,7},{7,8},{8,9},{9,10},{10,1... | collective-permute-start | bytes 786440 | tf_op jit(solution)/shard_map/ppermute | solution.py:27
  251.9 23.9 %copy-start.8 = (f32[2,2,256,256]{3,2,1,0:T(8,128)S(1)}, f32[2,2,256,256]{3,2,1,0:T(8,128)}, u32[]{:S(2)}) copy-start(f32[2,2,256,256]{3,2,1,0:T(8,128)} %param.16) | copy-start | bytes 3145732
  260.1 16.9 %copy-start.9 = (f32[2,256,256]{2,1,0:T(8,128)S(1)}, f32[2,256,256]{2,1,0:T(8,128)}, u32[]{:S(2)}) copy-start(f32[2,256,256]{2,1,0:T(8,128)} %get-tuple-element.66) | copy-start | bytes 1572868
  260.1 16.9 %copy-start.10 = (f32[2,256,256]{2,1,0:T(8,128)S(1)}, f32[2,256,256]{2,1,0:T(8,128)}, u32[]{:S(2)}) copy-start(f32[2,256,256]{2,1,0:T(8,128)} %get-tuple-element.67) | copy-start | bytes 1572868
  269.5 21.6 %collective-permute-start.8 = (f32[2,128,768]{2,1,0:T(8,128)}, f32[2,128,768]{2,1,0:T(8,128)}, u32[]{:S(2)}, u32[]{:S(2)}) collective-permute-start(f32[2,128,768]{2,1,0:T(8,128)} %get-tuple-element.93), channel_id=1, source_target_pairs={{16,0},{32,16},{48,32},{64,48},{80,64},{96,80},{112,96},{128,112},... | collective-permute-start | bytes 2359304 | tf_op jit(solution)/shard_map/ppermute | solution.py:27
  270.7 21.8 %collective-permute-start.9 = (f32[2,128,768]{2,1,0:T(8,128)}, f32[2,128,768]{2,1,0:T(8,128)}, u32[]{:S(2)}, u32[]{:S(2)}) collective-permute-start(f32[2,128,768]{2,1,0:T(8,128)} %get-tuple-element.92), channel_id=1, source_target_pairs={{0,16},{16,32},{32,48},{48,64},{64,80},{80,96},{96,112},{112,128},... | collective-permute-start | bytes 2359304 | tf_op jit(solution)/shard_map/ppermute | solution.py:27
  294.9 270.8 %collective-permute-start.10 = (bf16[2,512,128]{2,1,0:T(8,128)(2,1)}, bf16[2,512,128]{2,1,0:T(8,128)(2,1)}, u32[]{:S(2)}, u32[]{:S(2)}) collective-permute-start(bf16[2,512,128]{2,1,0:T(8,128)(2,1)} %get-tuple-element.101), channel_id=1, source_target_pairs={{1,0},{2,1},{3,2},{4,3},{5,4},{6,5},{7,6},{8,7},{9,8},{10,9},{11,1... | collective-permute-start | bytes 786440 | tf_op jit(solution)/shard_map/ppermute | solution.py:27
  297.5 269.4 %collective-permute-start.11 = (bf16[2,512,128]{2,1,0:T(8,128)(2,1)}, bf16[2,512,128]{2,1,0:T(8,128)(2,1)S(1)}, u32[]{:S(2)}, u32[]{:S(2)}) collective-permute-start(bf16[2,512,128]{2,1,0:T(8,128)(2,1)} %get-tuple-element.100), channel_id=1, source_target_pairs={{0,1},{1,2},{2,3},{3,4},{4,5},{5,6},{6,7},{7,8},{8,9},{9,10},{10,1... | collective-permute-start | bytes 786440 | tf_op jit(solution)/shard_map/ppermute | solution.py:27
  565.4 1.7 copy-start.5
Sparse Core Ops, SparseCore 0:
  278.2 284.8 all-reduce.1
where the time goes:
time: 582 us; the launch traced here: 576 us
  waiting for transfers between devices  283 us (49%)
  matrix products  107 us (18%)
  local copies, waits for them, and re-layouts  84.3 us (14%)
  between operations  38 us (7%)
  starting transfers between devices  35.4 us (6%)
  other arithmetic  28 us (5%)
    psum x1, waiting for transfers between devices, shards(): summed_terms = lax.psum(probe_parts, ('row', 'col'))  263 us
    dot_general x8, matrix products, right_product(): jnp.einsum('...kn,nm->...km', values, table, precision=highest_precision)  55.6 us
    dot_general x8, matrix products, left_product(): jnp.einsum('kn,...nm->...km', table, values, precision=highest_precision)  51.6 us
    dynamic_update_slice x6, local copies, waits for them, and re-layouts, shards(): lax.dynamic_update_slice(gradient, current + all_terms[slot_index], corne...  39.8 us
    gather x18, local copies, waits for them, and re-layouts  23 us
    ppermute x8, starting transfers between devices, passed_along(): lax.ppermute(value, axis, [(source, source + steps) for source in range(i...  22.1 us
  transfers between devices with their start and end apart: 13, of which 4 were waited for; matrix products, arithmetic and copies ran while one was open for 14% of the time, Pallas kernels for 0%

commit v1 on v0

v1 whole, which is shorter than its diff:
```python
import math

import jax
import jax.numpy as jnp
import ml_dtypes
import numpy as np
from jax import lax
from jax.experimental import pallas as pl
from jax.experimental.pallas import tpu as pltpu
from jax.sharding import PartitionSpec as P

MESH = pl.DeviceIdType.MESH
FR = 256
H = 128
TILE = 512
WIN = 768
OWN = 4
FRAMES = 6
F32 = jnp.float32
BF = jnp.bfloat16
I16 = jnp.int16

HALF = 4 * H + 16
STRIP = 8 * H + 16
CORNER = 2 * H + 16
PIECE = 64 + 16


def at_in(k):
    if k < 4:
        return k * HALF, HALF
    if k < 6:
        return 4 * HALF + (k - 4) * STRIP, STRIP
    return 4 * HALF + 2 * STRIP + (k - 6) * CORNER, CORNER


def view(ref, k):
    start, size = at_in(k)
    return ref.at[pl.ds(start, size)]


OUT_ROWS = 4 * HALF + 2 * STRIP
IN_ROWS = OUT_ROWS + 4 * CORNER


def code_of(largest):
    octaves = jnp.log(jnp.maximum(largest, 1e-30)) * (1.0 / math.log(2.0))
    return jnp.floor(16.0 * (14.98 - octaves))


def scale_of(code):
    return jnp.exp(code * (math.log(2.0) / 16.0))


def tall(tile, rows):
    return jnp.concatenate([tile] * (rows // 16), axis=0)


def encode(ref, places, values, code_at):
    largest = None
    for v in values:
        for t in range(0, v.shape[0], 16):
            a = jnp.abs(v[t : t + 16])
            largest = a if largest is None else jnp.maximum(largest, a)
    code = code_of(largest)
    scale = scale_of(code)
    for place, v in zip(places, values):
        rows = v.shape[0]
        ref[place : place + rows, :] = jnp.round(v * tall(scale, rows)).astype(jnp.int32).astype(I16)
    ref[code_at : code_at + 16, :] = code.astype(jnp.int32).astype(I16)


def scales(codes):
    return scale_of(-codes.astype(F32))


def greet(devices):
    barrier = pltpu.get_barrier_semaphore()
    for device in devices:
        pl.semaphore_signal(barrier, inc=1, device_id=device, device_id_type=MESH)


def remote(src, dst, send, recv, device):
    return pltpu.make_async_remote_copy(
        src_ref=src, dst_ref=dst, send_sem=send, recv_sem=recv, device_id=device, device_id_type=MESH
    )


def split(x):
    hi = x.astype(BF)
    return hi, (x - hi.astype(F32)).astype(BF)


def dot(a, b):
    return lax.dot_general(a, b, (((1,), (0,)), ((), ())), preferred_element_type=F32)


def left(table, x):
    (th, tl), (xh, xl) = table, split(x)
    return dot(th, xh) + (dot(th, xl) + dot(tl, xh))


def right(x, table):
    (th, tl), (xh, xl) = table, split(x)
    return dot(xh, th) + (dot(xl, th) + dot(xh, tl))


def kernel(
    obj_ref, probe_ref, own_pos, lend_pos, lend_live, own_amp, recv_amp, th_ref, tl_ref, perm_ref,
    stage, grad_ref,
    win, probe, th, tl, perm, amp, lent, amp_sorted, terms, pg, where, live_of,
    out1, in1, relay1, out2, in2, relay2, edge,
    from_core, half, spread, pieces, deep_all, gathered,
    local, send1, recv1, send2, recv2, asend, arecv,
):
    row, col = lax.axis_index("row"), lax.axis_index("col")
    x, zl, core = lax.div(col, 4), lax.rem(lax.div(col, 2), 2), lax.rem(col, 2)
    zh, y = lax.div(row, 4), lax.rem(row, 4)
    plane, deep = x * 4 + y, zh * 2 + zl

    def dev(dr, dc):
        return (lax.rem(row + (16 + dr), 16), lax.rem(col + (16 + dc), 16))

    twin = (row, col + 1 - 2 * core)
    flat = []
    for d in range(1, 16):
        tx, ty = lax.rem(x + d // 4, 4), lax.rem(y + d % 4, 4)
        fx, fy = lax.rem(x + 4 - d // 4, 4), lax.rem(y + 4 - d % 4, 4)
        flat.append(((zh * 4 + ty, tx * 4 + zl * 2 + core), tx * 4 + ty, fx * 4 + fy))
    high = []
    for d in range(1, 8):
        there = lax.rem(deep + d, 8)
        high.append((lax.div(there, 2) * 4 + y, x * 4 + lax.rem(there, 2) * 2 + core))

    partners = [dev(*d) for d in ((1, 0), (-1, 0), (0, 1), (0, -1), (4, 0), (-4, 0), (3, 0), (-3, 0))]
    partners += [twin] + [f[0] for f in flat] + high
    greet(partners)
    loads = []
    for p in range(2):
        for j in range(4):
            loads.append((obj_ref.at[p, :, pl.ds(j * H, H)], win.at[p, j + 1, pl.ds(H, TILE), :]))
    loads += [(probe_ref, probe), (own_amp, amp), (perm_ref, perm), (th_ref, th), (tl_ref, tl)]
    loads = [pltpu.make_async_copy(s, d, local.at[k]) for k, (s, d) in enumerate(loads)]
    for copy in loads:
        copy.start()

    for k in range(OWN):
        where[2 * k] = jnp.clip(own_pos[0, k] - row * TILE + H, 0, TILE)
        where[2 * k + 1] = jnp.clip(own_pos[1, k] - col * TILE + H, 0, TILE)
        live_of[k] = jnp.float32(1.0)
    for k in range(FRAMES - OWN):
        where[2 * (OWN + k)] = jnp.clip(lend_pos[k, 0] - row * TILE + H, 0, TILE)
        where[2 * (OWN + k) + 1] = jnp.clip(lend_pos[k, 1] - col * TILE + H, 0, TILE)
        live_of[OWN + k] = lend_live[k].astype(F32)

    for copy in loads[:8]:
        copy.wait()

    def of_win(i, j):
        return [win[p, j + 1, (i + 1) * H : (i + 2) * H, :] for p in range(2)]

    def put_half(ref, k, blocks, code_mid):
        base = at_in(k)[0]
        values = [v for b in blocks for v in b]
        if code_mid:
            places, code_at = [base, base + H, base + 272, base + 272 + H], base + 256
        else:
            places, code_at = [base, base + H, base + 256, base + 256 + H], base + 512
        encode(ref, places, values, code_at)

    def put_strip(ref, k, blocks):
        base = at_in(k)[0]
        values = [v for b in blocks for v in b]
        encode(ref, [base + H * t for t in range(8)], values, base + 8 * H)

    put_half(out1, 1, [of_win(3, 1), of_win(3, 2)], False)
    put_half(out1, 3, [of_win(0, 1), of_win(0, 2)], False)
    put_half(out1, 0, [of_win(3, 0), of_win(3, 3)], True)
    put_half(out1, 2, [of_win(0, 0), of_win(0, 3)], True)
    put_strip(out1, 4, [of_win(i, 0) for i in range(4)])
    put_strip(out1, 5, [of_win(i, 3) for i in range(4)])
    pl.semaphore_wait(pltpu.get_barrier_semaphore(), len(partners))

    class Exchange:
        def __init__(self, out, inn, relay, send, recv):
            def go(k, there, device):
                return remote(view(out, k), view(inn, there), send.at[k], recv.at[there], device)

            self.down = [go(0, 0, dev(1, 0)), go(1, 1, dev(1, 0))]
            self.up = [go(2, 2, dev(-1, 0)), go(3, 3, dev(-1, 0))]
            self.lefts = go(4, 5, dev(0, -1))
            self.rights = go(5, 4, dev(0, 1))
            self.relays = [
                remote(view(out, 1), relay.at[0], send.at[1], recv.at[10], dev(-3, 0)),
                remote(view(out, 3), relay.at[1], send.at[3], recv.at[11], dev(3, 0)),
            ]
            self.onward = [
                remote(relay.at[0], view(inn, 1), send.at[10], recv.at[1], dev(4, 0)),
                remote(relay.at[1], view(inn, 3), send.at[11], recv.at[3], dev(-4, 0)),
            ]

        def start_second_halves(self):
            for turn, direct, relayed in ((3, self.down[1], self.relays[0]), (0, self.up[1], self.relays[1])):
                pl.when(y == turn)(relayed.start)
                pl.when(y != turn)(direct.start)

        def pass_on(self):
            for turn, k in ((0, 0), (3, 1)):

                def onward(k=k):
                    self.relays[k].wait_recv()
                    self.onward[k].start()

                pl.when(y == turn)(onward)

        def finish_sends(self):
            for copy in self.down + self.up + [self.lefts, self.rights]:
                copy.wait_send()
            pl.when(y == 0)(self.onward[0].wait_send)
            pl.when(y == 3)(self.onward[1].wait_send)

    first = Exchange(out1, in1, relay1, send1, recv1)
    first.start_second_halves()
    first.down[0].start()
    first.up[0].start()
    first.lefts.start()
    first.rights.start()
    lends = [
        remote(recv_amp.at[0], lent.at[0], asend.at[46], arecv.at[46], dev(0, -1)),
        remote(recv_amp.at[1], lent.at[1], asend.at[47], arecv.at[47], dev(0, 1)),
    ]

    for copy in loads[8:]:
        copy.wait()
    pg[...] = jnp.zeros_like(pg)
    edges = jnp.zeros((H, H), F32)

    def clear(f, carry):
        for p in range(2):
            for k in range(3):
                terms[f, p, k, :H, :] = edges
                terms[f, p, k, H + FR :, :] = edges
        return carry

    lax.fori_loop(0, FRAMES, clear, 0)
    first.pass_on()
    power = sum(probe[m, q] ** 2 for m in range(2) for q in range(2))
    inverse = 1.0 / (jnp.full((1, H), jnp.max(power), F32) + 1e-6)

    def sort_own(f, carry):
        amp_sorted[f] = dot(dot(perm[0], amp[f]).astype(BF), perm[1]).astype(BF)
        return carry

    lax.fori_loop(0, OWN, sort_own, 0)

    def open_blocks(ref, k, spots, first_at, code_at):
        base = at_in(k)[0]
        scale = tall(scales(ref[base + code_at : base + code_at + 16, :]), H)
        out = []
        for spot, at in zip(spots, first_at):
            out.append((spot, [ref[base + at + p * H : base + at + (p + 1) * H, :].astype(F32) * scale for p in range(2)]))
        return out

    def fill(k, spots, first_at, code_at):
        for (i, j), planes in open_blocks(in1, k, spots, first_at, code_at):
            for p in range(2):
                win[p, j, i * H : (i + 1) * H, :] = planes[p]

    corners = [
        (0, 0, 7, -1, 0), (0, 256, 6, 1, 1), (2, 0, 9, -1, 2), (2, 256, 8, 1, 3),
    ]
    forwards = []
    for k, at, there, side, n in corners:
        src = in1.at[pl.ds(at_in(k)[0] + at, CORNER)]
        forwards.append(remote(src, view(in1, there), send1.at[6 + n], recv1.at[there], dev(0, side)))
    first.down[0].wait_recv()
    forwards[0].start()
    forwards[1].start()
    first.up[0].wait_recv()
    forwards[2].start()
    forwards[3].start()
    fill(0, [(0, 1), (0, 4)], [0, 272], 256)
    fill(2, [(5, 1), (5, 4)], [0, 272], 256)
    first.rights.wait_recv()
    fill(4, [(i, 0) for i in range(1, 5)], [256 * t for t in range(4)], 1024)
    first.lefts.wait_recv()
    fill(5, [(i, 5) for i in range(1, 5)], [256 * t for t in range(4)], 1024)
    first.down[1].wait_recv()
    fill(1, [(0, 2), (0, 3)], [0, 256], 512)
    first.up[1].wait_recv()
    fill(3, [(5, 2), (5, 3)], [0, 256], 512)
    for n, (k, spot) in enumerate(((7, (0, 5)), (6, (0, 0)), (9, (5, 5)), (8, (5, 0)))):
        forwards[n].wait_recv()
        fill(k, [spot], [0 if n % 2 == 0 else 16], 256 if n % 2 == 0 else 0)
    for copy in lends:
        copy.start()
    lane = lax.broadcasted_iota(jnp.int32, (FR, H), 1)

    T = [(th[g], tl[g]) for g in range(2)]
    Tt = [(th[2 + g], tl[2 + g]) for g in range(2)]

    def two(ff, carry):
        S=[]; P={}; e={}; cols={}
        for u in range(2):
            f=2*ff+u
            r=where[2*f]; c=where[2*f+1]
            cb=lax.div(c,H); s=c-cb*H
            live=live_of[f]
            S.append((f,r,cb,s))
            for p in range(2):
                R=[pltpu.roll(win[p,jnp.minimum(cb+k,5),pl.ds(r,FR),:],lax.rem(H-s,H),axis=1) for k in range(3)]
                for h in range(2): P[u,p,h]=jnp.where(lane<H-s,R[h],R[h+1])*live
            for m in range(2):
                for h in range(2):
                    pr=probe[m,0,:,h*H:(h+1)*H]; pi=probe[m,1,:,h*H:(h+1)*H]
                    e[u,m,0,h]=pr*P[u,0,h]-pi*P[u,1,h]; e[u,m,1,h]=pr*P[u,1,h]+pi*P[u,0,h]
                for g in range(2):
                    a=[e[u,m,q,0]+e[u,m,q,1] if g==0 else e[u,m,q,0]-e[u,m,q,1] for q in range(2)]
                    cols[u,m,g]=right(jnp.concatenate(a,axis=1),Tt[g])
        far={}
        for u in range(2):
            for m in range(2):
                for g in range(2):
                    x=[]
                    for q in range(2):
                        whole=jnp.concatenate([cols[u,m,0][:,q*H:(q+1)*H],cols[u,m,1][:,q*H:(q+1)*H]],axis=1)
                        x.append(whole[:H]+whole[H:] if g==0 else whole[:H]-whole[H:])
                    far[u,m,g]=left(T[g],jnp.concatenate(x,axis=0))
        B={}
        for u in range(2):
            A=amp_sorted[S[u][0]].astype(F32)
            for g in range(2):
                power=sum(far[u,m,g][:H]**2+far[u,m,g][H:]**2 for m in range(2))
                keep=1.0-A[g*H:(g+1)*H]*lax.rsqrt(jnp.maximum(power,1.0))
                kk=jnp.concatenate([keep,keep],axis=0)
                for m in range(2):
                    B[u,m,g]=left(Tt[g],far[u,m,g]*kk)
        D={}
        for u in range(2):
            for m in range(2):
                z=[]
                for q in range(2):
                    a=B[u,m,0][q*H:(q+1)*H]; b=B[u,m,1][q*H:(q+1)*H]
                    z.append(jnp.concatenate([a+b,a-b],axis=0))
                for g in range(2):
                    D[u,m,g]=right(jnp.concatenate([z[0][:,g*H:(g+1)*H],z[1][:,g*H:(g+1)*H]],axis=1),T[g])
        o={}
        for u in range(2):
          for m in range(2):
            for h in range(2):
                br,bi=[ (D[u,m,0][:,q*H:(q+1)*H]+D[u,m,1][:,q*H:(q+1)*H]) if h==0 else (D[u,m,0][:,q*H:(q+1)*H]-D[u,m,1][:,q*H:(q+1)*H]) for q in range(2)]
                pr=probe[m,0,:,h*H:(h+1)*H]; pi=probe[m,1,:,h*H:(h+1)*H]
                x0=pr*br+pi*bi; x1=pr*bi-pi*br
                o[u,0,h]=x0 if m==0 else o[u,0,h]+x0
                o[u,1,h]=x1 if m==0 else o[u,1,h]+x1
                pg[pl.ds((m*2*2+h)*FR,FR),:]+=P[u,0,h]*br+P[u,1,h]*bi
                pg[pl.ds(((m*2+1)*2+h)*FR,FR),:]+=P[u,0,h]*bi-P[u,1,h]*br
        for u in range(2):
          f,r,cb,s=S[u]
          for p in range(2):
            R0=pltpu.roll(o[u,p,0],s,axis=1); R1=pltpu.roll(o[u,p,1],s,axis=1)
            low=lane<s
            blk=[jnp.where(low,0.0,R0),jnp.where(low,R0,R1),jnp.where(low,R1,0.0)]
            for k in range(3):
                terms[f,p,k,H:H+FR,:]=blk[k]
        return carry
    def each(f, carry):
        def lent_frames():
            for k in range(2):
                lends[k].wait_recv()
                amp_sorted[OWN + k] = dot(dot(perm[0], lent[k]).astype(BF), perm[1]).astype(BF)

        pl.when(f == OWN // 2)(lent_frames)
        return two(f, carry)

    lax.fori_loop(0, FRAMES // 2, each, 0)

    def at_rows(ref, index, rows):
        return ref.at[pl.ds(pl.multiple_of(index * rows, rows), rows)]

    swap = remote(at_rows(pg, 1 - core, 1024), from_core, asend.at[0], arecv.at[0], twin)
    swap.start()

    spots = [(where[2 * f], lax.div(where[2 * f + 1], H)) for f in range(FRAMES)]

    def block(i, j):
        planes = []
        for p in range(2):
            total = None
            for f, (r, cb) in enumerate(spots):
                k = j - cb
                at = jnp.where((k < 0) | (k > 2), 0, jnp.clip(i * H - r, -H, FR) + H)
                k = jnp.clip(k, 0, 2)
                part = terms[f, p, k, pl.ds(at, H), :]
                total = part if total is None else total + part
            planes.append(total * inverse)
        return planes

    second = Exchange(out2, in2, relay2, send2, recv2)
    base = OUT_ROWS
    aside = []
    for n, (j, side) in enumerate(((0, -1), (5, 1))):
        at = base + n * HALF
        encode(out2, [at, at + H, at + 256, at + 256 + H], block(0, j) + block(5, j), at + 512)
        there = base + (1 - n) * HALF
        aside.append(
            remote(out2.at[pl.ds(at, HALF)], in2.at[pl.ds(there, HALF)], send2.at[6 + n], recv2.at[7 - n], dev(0, side))
        )
        aside[-1].start()
    put_half(out2, 1, [block(5, 2), block(5, 3)], False)
    put_half(out2, 3, [block(0, 2), block(0, 3)], False)
    second.start_second_halves()

    swap.wait()
    half[...] = pg[pl.ds(pl.multiple_of(core * 1024, 1024), 1024), :] + from_core[...]
    def spread_out(k, carry):
        value = half[pl.ds(pl.multiple_of(k * 64, 64), 64), :]
        largest = jnp.abs(value[:16])
        for t in range(16, 64, 16):
            largest = jnp.maximum(largest, jnp.abs(value[t : t + 16]))
        code = code_of(largest)
        spread[k, :64, :] = jnp.round(value * tall(scale_of(code), 64)).astype(jnp.int32).astype(I16)
        spread[k, 64:, :] = code.astype(jnp.int32).astype(I16)
        return carry

    lax.fori_loop(0, 16, spread_out, 0)
    scatter = []
    for d, (device, there, _) in enumerate(flat):
        scatter.append(remote(spread.at[there], pieces.at[d], asend.at[1 + d], arecv.at[1 + d], device))
        scatter[-1].start()

    put_strip(out2, 4, [block(i, 0) for i in range(1, 5)])
    second.lefts.start()
    put_strip(out2, 5, [block(i, 5) for i in range(1, 5)])
    second.rights.start()
    for n, (i, j) in enumerate(((0, 1), (0, 4), (5, 1), (5, 4))):
        planes = block(i, j)
        for p in range(2):
            edge[n, p] = planes[p]
    second.pass_on()
    for n in range(2):
        aside[n].wait_recv()
    sums = {}
    for n, j in ((0, 1), (1, 4)):
        at = base + n * HALF
        scale = tall(scales(in2[at + 512 : at + 528, :]), H)
        for i, off, e in ((0, 0, n), (5, 256, 2 + n)):
            sums[(i, j)] = [edge[e, p] + in2[at + off + p * H : at + off + (p + 1) * H, :].astype(F32) * scale for p in range(2)]
    put_half(out2, 2, [sums[(0, 1)], sums[(0, 4)]], False)
    second.up[0].start()
    put_half(out2, 0, [sums[(5, 1)], sums[(5, 4)]], False)
    second.down[0].start()

    def piece_of(ref, k):
        return ref[k, :64, :].astype(F32) * tall(scales(ref[k, 64:, :]), 64)

    def put_piece(ref, k, value):
        largest = jnp.abs(value[:16])
        for t in range(16, 64, 16):
            largest = jnp.maximum(largest, jnp.abs(value[t : t + 16]))
        code = code_of(largest)
        ref[k, :64, :] = jnp.round(value * tall(scale_of(code), 64)).astype(jnp.int32).astype(I16)
        ref[k, 64:, :] = code.astype(jnp.int32).astype(I16)

    for copy in scatter:
        copy.wait()
    total = half[pl.ds(pl.multiple_of(plane * 64, 64), 64), :]
    for d in range(15):
        total = total + piece_of(pieces, d)
    put_piece(deep_all, deep, total)
    depth = []
    for d, device in enumerate(high):
        depth.append(remote(deep_all.at[deep], deep_all.at[deep], asend.at[16 + d], arecv.at[16 + d], device))
        depth[-1].start()

    for i in range(4):
        for j in range(4):
            planes = block(i + 1, j + 1)
            for p in range(2):
                stage[p, i * H : (i + 1) * H, j * H : (j + 1) * H] = win[p, j + 1, (i + 1) * H : (i + 2) * H, :] - planes[p]

    for copy in depth:
        copy.wait()
    total = piece_of(deep_all, 0)
    for k in range(1, 8):
        total = total + piece_of(deep_all, k)
    put_piece(gathered, core * 16 + plane, total * (1.0 / 1024.0))
    gather = []
    mine = gathered.at[core * 16 + plane]
    for d, (device, _, _) in enumerate(flat):
        gather.append(remote(mine, mine, asend.at[23 + d], arecv.at[23 + d], device))
        gather[-1].start()
    cross = [remote(mine, mine, asend.at[38], arecv.at[38], twin)]
    cross[0].start()

    def take(k, spots, first_at, code_at):
        for (i, j), planes in open_blocks(in2, k, spots, first_at, code_at):
            for p in range(2):
                spot = (p, slice(i * H, (i + 1) * H), slice(j * H, (j + 1) * H))
                stage[spot] = stage[spot] - planes[p]

    for d, (_, _, origin) in enumerate(flat):
        gather[d].wait_recv()
        part = gathered.at[core * 16 + origin]
        cross.append(remote(part, part, asend.at[48 + d], arecv.at[48 + d], twin))
        cross[-1].start()

    second.rights.wait_recv()
    take(4, [(i, 0) for i in range(4)], [256 * t for t in range(4)], 1024)
    second.lefts.wait_recv()
    take(5, [(i, 3) for i in range(4)], [256 * t for t in range(4)], 1024)

    second.down[1].wait_recv()
    take(1, [(0, 1), (0, 2)], [0, 256], 512)
    second.up[1].wait_recv()
    take(3, [(3, 1), (3, 2)], [0, 256], 512)
    second.down[0].wait_recv()
    take(0, [(0, 0), (0, 3)], [0, 256], 512)
    second.up[0].wait_recv()
    take(2, [(3, 0), (3, 3)], [0, 256], 512)

    def spell(k, carry):
        value = gathered[k, :64, :].astype(F32) * tall(scales(gathered[k, 64:, :]), 64)
        m, q, h, part = lax.div(k, 16), lax.rem(lax.div(k, 8), 2), lax.rem(lax.div(k, 4), 2), lax.rem(k, 4)
        grad_ref[m, q, pl.ds(pl.multiple_of(part * 64, 64), 64), pl.ds(pl.multiple_of(h * H, H), H)] = value
        return carry

    for copy in cross:
        copy.wait_recv()
    lax.fori_loop(0, 32, spell, 0)
    first.finish_sends()
    second.finish_sends()
    for copy in forwards + lends + aside + gather + cross:
        copy.wait_send()


def tables():
    n = np.arange(FR)
    angles = (n[:, None] * n[None, :] % FR) * (2.0 * math.pi / FR)
    cosine, sine = np.cos(angles) / 16.0, np.sin(angles) / 16.0
    both = []
    for g in range(2):
        c, s = cosine[g::2, :H], sine[g::2, :H]
        both.append(np.block([[c, s], [-s, c]]))
    both = np.stack(both + [b.T for b in both])
    hi = both.astype(np.float32).astype(ml_dtypes.bfloat16)
    lo = (both - hi.astype(np.float64)).astype(np.float32).astype(ml_dtypes.bfloat16)
    order = np.zeros((FR, FR), np.float32)
    order[np.arange(FR), np.concatenate([n[0::2], n[1::2]])] = 1.0
    return hi, lo, np.stack([order, order.T]).astype(ml_dtypes.bfloat16)


def shards(object_field, probe, own_pos, own_amp, lend_pos, lend_live, recv_amp):
    sm = pl.BlockSpec(memory_space=pltpu.SMEM)
    hbm = pl.BlockSpec(memory_space=pl.ANY)
    dma = pltpu.SemaphoreType.DMA
    hi, lo, order = tables()

    def vm(shape, dtype=F32):
        return pltpu.VMEM(shape, dtype)

    args = (object_field, probe, own_pos.T, lend_pos, lend_live, own_amp, recv_amp, jnp.asarray(hi), jnp.asarray(lo), jnp.asarray(order))
    held = [pltpu.with_memory_space_constraint(a, pltpu.HBM) for a in args]
    return pl.pallas_call(
        kernel,
        out_shape=(
            jax.ShapeDtypeStruct(object_field.shape, F32),
            jax.ShapeDtypeStruct(probe.shape, F32),
        ),
        in_specs=[hbm, hbm, sm, sm, sm, hbm, hbm, hbm, hbm, hbm],
        out_specs=(pl.BlockSpec(memory_space=pltpu.VMEM),) * 2,
        scratch_shapes=[
            vm((2, 6, WIN, H)),
            vm((2, 2, FR, FR)),
            vm((4, FR, FR), BF),
            vm((4, FR, FR), BF),
            vm((2, FR, FR), BF),
            vm((OWN, FR, FR), BF),
            vm((FRAMES - OWN, FR, FR), BF),
            vm((FRAMES, FR, FR), BF),
            vm((FRAMES, 2, 3, 2 * FR, H)),
            vm((2048, H)),
            pltpu.SMEM((2 * FRAMES,), jnp.int32),
            pltpu.SMEM((FRAMES,), F32),
            vm((OUT_ROWS, H), I16),
            vm((IN_ROWS, H), I16),
            vm((2, HALF, H), I16),
            vm((OUT_ROWS + 2 * HALF, H), I16),
            vm((OUT_ROWS + 2 * HALF, H), I16),
            vm((2, HALF, H), I16),
            vm((4, 2, H, H)),
            vm((1024, H)),
            vm((1024, H)),
            vm((16, PIECE, H), I16),
            vm((15, PIECE, H), I16),
            vm((8, PIECE, H), I16),
            vm((32, PIECE, H), I16),
            dma((13,)),
            dma((12,)),
            dma((12,)),
            dma((12,)),
            dma((12,)),
            dma((63,)),
            dma((63,)),
        ],
        compiler_params=pltpu.CompilerParams(collective_id=0, has_side_effects=True, vmem_limit_bytes=46 << 20),
        name="step",
    )(*held)


def solution(mesh):
    placed = (
        P(None, "row", "col"),
        P(),
        P(("row", "col"), None),
        P(("row", "col"), None, None),
        P(("row", "col"), None),
        P(("row", "col")),
        P(("row", "col"), None, None),
    )
    return jax.shard_map(
        shards, mesh=mesh, in_specs=placed, out_specs=(P(None, "row", "col"), P()), check_vma=False
    )
```

time: 582 us -> 76.7 us (0.13); the launches traced: 576 us -> 76.6 us
  waiting for transfers between devices: 283 us -> 0 us
  matrix products: 107 us -> 0 us
  local copies, waits for them, and re-layouts: 84.3 us -> 2.29 us
  Pallas kernels: 0 us -> 73.6 us
  between operations: 38 us -> 0.64 us
  starting transfers between devices: 35.4 us -> 0 us
  other arithmetic: 28 us -> 0 us
    psum x1 -> x0, waiting for transfers between devices: 263 us -> none  [shards(): summed_terms = lax.psum(probe_parts, ('row', 'col'))]
    dot_general x16 -> x0, matrix products: 107 us -> none  [the longest x8 55.6 us: right_product(): jnp.einsum('...kn,nm->...km', values, table, precision=highest_precision)]
    pallas_call x0 -> x1, Pallas kernels: none -> 73.6 us  [shards(): pl.pallas_call(kernel, out_shape=(jax.ShapeDtypeStruct(object_field.shape...]
    dynamic_update_slice x6 -> x0, local copies, waits for them, and re-layouts: 39.8 us -> none  [shards(): lax.dynamic_update_slice(gradient, current + all_terms[slot_index], corne...]
    ppermute x12 -> x0, starting transfers between devices: 35.4 us -> none  [the longest x8 22.1 us: passed_along(): lax.ppermute(value, axis, [(source, source + steps) for source in range(i...]
    gather x18 -> x0, local copies, waits for them, and re-layouts: 23 us -> none
    ppermute x12 -> x0, waiting for transfers between devices: 19.8 us -> none  [the longest x8 10.8 us: passed_along(): lax.ppermute(value, axis, [(source, source + steps) for source in range(i...]
    slice x10 -> x0, local copies, waits for them, and re-layouts: 11.9 us -> none  [the longest x1 2.71 us: shards(): from_above = pass_rows(gradient[:, half_width + tile_len:], 1)]
  transfers between devices with their start and end apart: 13 -> 0, of which waited for: 4 -> 0; matrix products, arithmetic and copies ran while one was open for 14% -> 0% of each run, Pallas kernels for 0% -> 0%
where the time goes in v1:
time: 76.7 us; the launch traced here: 76.6 us
  Pallas kernels  73.6 us (96%)
  local copies, waits for them, and re-layouts  2.29 us (3%)
    pallas_call x1, Pallas kernels, shards(): pl.pallas_call(kernel, out_shape=(jax.ShapeDtypeStruct(object_field.shape...  73.6 us
    unnamed x2, local copies, waits for them, and re-layouts  2.29 us

profile of v1, /device:TPU:1, one launch (start us, length us, event | category | flops | bytes accessed | tf_op | source)
XLA Modules:
  0.0 76.6 jit_solution(964040432981513190)
XLA Ops:
  0.6 73.6 %step.1 = (f32[2,512,512]{2,1,0:T(8,128)S(1)}, f32[2,2,256,256]{3,2,1,0:T(8,128)S(1)}) custom-call(f32[2,512,512]{2,1,0:T(8,128)} %obj_ref.1, f32[2,2,256,256]{3,2,1,0:T(8,128)} %probe_ref.1, s32[2,4]{1,0:T(2,128)} %bitcast.1, s32[2,2]{1,0:T(2,128)} %lend_pos.1, s32[2]{0:T(128)} %lend_live.1, bf16[4,256,256]{2,1,0:T(8,128)(2,1)} %own_amp.1, ...), custom_call_target="tpu_custom_call" | custom-call | tf_op jit(solution)/shard_map/step/pallas_call | solution.py:564
  74.3 1.3 %copy.14 = f32[2,512,512]{2,1,0:T(8,128)} copy(f32[2,512,512]{2,1,0:T(8,128)S(1)} %get-tuple-element.4) | data formatting | bytes 4194304
  75.6 1.0 %copy.15 = f32[2,2,256,256]{3,2,1,0:T(8,128)} copy(f32[2,2,256,256]{3,2,1,0:T(8,128)S(1)} %get-tuple-element.5) | data formatting | bytes 2097152

commit v2 on v1

--- a/solution.py
+++ b/solution.py
@@ -22,16 +22,20 @@
 
 HALF = 4 * H + 16
 STRIP = 8 * H + 16
-CORNER = 2 * H + 16
+BLOCK = 2 * H + 16
 PIECE = 64 + 16
 
 
 def at_in(k):
-    if k < 4:
-        return k * HALF, HALF
-    if k < 6:
-        return 4 * HALF + (k - 4) * STRIP, STRIP
-    return 4 * HALF + 2 * STRIP + (k - 6) * CORNER, CORNER
+    if k < 8:
+        return k * BLOCK, BLOCK
+    if k < 10:
+        return 8 * BLOCK + (k - 8) * STRIP, STRIP
+    return 8 * BLOCK + 2 * STRIP + (k - 10) * BLOCK, BLOCK
+
+
+COLUMNS = (0, 3, 1, 2)
+ROUTES = {1: (-3, 4, 0), 2: (-1, 2, 2), 3: (-2, 3, 1)}
 
 
 def view(ref, k):
@@ -39,8 +43,8 @@
     return ref.at[pl.ds(start, size)]
 
 
-OUT_ROWS = 4 * HALF + 2 * STRIP
-IN_ROWS = OUT_ROWS + 4 * CORNER
+OUT_ROWS = 8 * BLOCK + 2 * STRIP
+IN_ROWS = OUT_ROWS + 4 * BLOCK
 
 
 def code_of(largest):
@@ -132,7 +136,7 @@
         there = lax.rem(deep + d, 8)
         high.append((lax.div(there, 2) * 4 + y, x * 4 + lax.rem(there, 2) * 2 + core))
 
-    partners = [dev(*d) for d in ((1, 0), (-1, 0), (0, 1), (0, -1), (4, 0), (-4, 0), (3, 0), (-3, 0))]
+    partners = [dev(*d) for d in ((1, 0), (-1, 0), (0, 1), (0, -1), (2, 0), (-2, 0), (3, 0), (-3, 0), (4, 0), (-4, 0))]
     partners += [twin] + [f[0] for f in flat] + high
     greet(partners)
     loads = []
@@ -159,26 +163,20 @@
     def of_win(i, j):
         return [win[p, j + 1, (i + 1) * H : (i + 2) * H, :] for p in range(2)]
 
-    def put_half(ref, k, blocks, code_mid):
+    def put_block(ref, k, planes):
         base = at_in(k)[0]
-        values = [v for b in blocks for v in b]
-        if code_mid:
-            places, code_at = [base, base + H, base + 272, base + 272 + H], base + 256
-        else:
-            places, code_at = [base, base + H, base + 256, base + 256 + H], base + 512
-        encode(ref, places, values, code_at)
+        encode(ref, [base, base + H], planes, base + 2 * H)
 
     def put_strip(ref, k, blocks):
         base = at_in(k)[0]
         values = [v for b in blocks for v in b]
         encode(ref, [base + H * t for t in range(8)], values, base + 8 * H)
 
-    put_half(out1, 1, [of_win(3, 1), of_win(3, 2)], False)
-    put_half(out1, 3, [of_win(0, 1), of_win(0, 2)], False)
-    put_half(out1, 0, [of_win(3, 0), of_win(3, 3)], True)
-    put_half(out1, 2, [of_win(0, 0), of_win(0, 3)], True)
-    put_strip(out1, 4, [of_win(i, 0) for i in range(4)])
-    put_strip(out1, 5, [of_win(i, 3) for i in range(4)])
+    for q in (3, 2, 1, 0):
+        put_block(out1, q, of_win(3, COLUMNS[q]))
+        put_block(out1, 4 + q, of_win(0, COLUMNS[q]))
+    put_strip(out1, 8, [of_win(i, 0) for i in range(4)])
+    put_strip(out1, 9, [of_win(i, 3) for i in range(4)])
     pl.semaphore_wait(pltpu.get_barrier_semaphore(), len(partners))
 
     class Exchange:
@@ -186,43 +184,45 @@
             def go(k, there, device):
                 return remote(view(out, k), view(inn, there), send.at[k], recv.at[there], device)
 
-            self.down = [go(0, 0, dev(1, 0)), go(1, 1, dev(1, 0))]
-            self.up = [go(2, 2, dev(-1, 0)), go(3, 3, dev(-1, 0))]
-            self.lefts = go(4, 5, dev(0, -1))
-            self.rights = go(5, 4, dev(0, 1))
-            self.relays = [
-                remote(view(out, 1), relay.at[0], send.at[1], recv.at[10], dev(-3, 0)),
-                remote(view(out, 3), relay.at[1], send.at[3], recv.at[11], dev(3, 0)),
-            ]
-            self.onward = [
-                remote(relay.at[0], view(inn, 1), send.at[10], recv.at[1], dev(4, 0)),
-                remote(relay.at[1], view(inn, 3), send.at[11], recv.at[3], dev(-4, 0)),
-            ]
-
-        def start_second_halves(self):
-            for turn, direct, relayed in ((3, self.down[1], self.relays[0]), (0, self.up[1], self.relays[1])):
-                pl.when(y == turn)(relayed.start)
-                pl.when(y != turn)(direct.start)
-
-        def pass_on(self):
-            for turn, k in ((0, 0), (3, 1)):
-
-                def onward(k=k):
-                    self.relays[k].wait_recv()
-                    self.onward[k].start()
-
-                pl.when(y == turn)(onward)
+            self.down = [go(q, q, dev(1, 0)) for q in range(4)]
+            self.up = [go(4 + q, 4 + q, dev(-1, 0)) for q in range(4)]
+            self.lefts = go(8, 9, dev(0, -1))
+            self.rights = go(9, 8, dev(0, 1))
+            self.routes = {}
+            for q, (there, onward, at_y) in ROUTES.items():
+                for way, sign, turn, k in ((0, 1, 3, q), (1, -1, 0, 4 + q)):
+                    hop = remote(view(out, k), relay.at[way], send.at[k], recv.at[14 + way], dev(sign * there, 0))
+                    rest = remote(relay.at[way], view(inn, k), send.at[14 + way], recv.at[k], dev(sign * onward, 0))
+                    self.routes[q, way] = (turn, hop, at_y if way == 0 else 3 - at_y, rest)
+
+        def start(self, q):
+            for way, direct in ((0, self.down[q]), (1, self.up[q])):
+                if q == 0:
+                    direct.start()
+                else:
+                    turn, hop, _, _ = self.routes[q, way]
+                    pl.when(y == turn)(hop.start)
+                    pl.when(y != turn)(direct.start)
+
+        def pass_on(self, q):
+            for way in range(2):
+                _, hop, at_y, rest = self.routes[q, way]
+
+                def onward(hop=hop, rest=rest):
+                    hop.wait_recv()
+                    rest.start()
+
+                pl.when(y == at_y)(onward)
 
         def finish_sends(self):
             for copy in self.down + self.up + [self.lefts, self.rights]:
                 copy.wait_send()
-            pl.when(y == 0)(self.onward[0].wait_send)
-            pl.when(y == 3)(self.onward[1].wait_send)
+            pl.when(y != 3)(self.routes[1, 0][3].wait_send)
+            pl.when(y != 0)(self.routes[1, 1][3].wait_send)
 
     first = Exchange(out1, in1, relay1, send1, recv1)
-    first.start_second_halves()
-    first.down[0].start()
-    first.up[0].start()
+    for q in (3, 2, 1, 0):
+        first.start(q)
     first.lefts.start()
     first.rights.start()
     lends = [
@@ -243,7 +243,8 @@
         return carry
 
     lax.fori_loop(0, FRAMES, clear, 0)
-    first.pass_on()
+    for q in (3, 2, 1):
+        first.pass_on(q)
     power = sum(probe[m, q] ** 2 for m in range(2) for q in range(2))
     inverse = 1.0 / (jnp.full((1, H), jnp.max(power), F32) + 1e-6)
 
@@ -253,45 +254,41 @@
 
     lax.fori_loop(0, OWN, sort_own, 0)
 
-    def open_blocks(ref, k, spots, first_at, code_at):
-        base = at_in(k)[0]
-        scale = tall(scales(ref[base + code_at : base + code_at + 16, :]), H)
+    def open_blocks(ref, k, spots):
+        base, size = at_in(k)
+        scale = tall(scales(ref[base + size - 16 : base + size, :]), H)
         out = []
-        for spot, at in zip(spots, first_at):
-            out.append((spot, [ref[base + at + p * H : base + at + (p + 1) * H, :].astype(F32) * scale for p in range(2)]))
+        for n, spot in enumerate(spots):
+            at = base + 2 * H * n
+            out.append((spot, [ref[at + p * H : at + (p + 1) * H, :].astype(F32) * scale for p in range(2)]))
         return out
 
-    def fill(k, spots, first_at, code_at):
-        for (i, j), planes in open_blocks(in1, k, spots, first_at, code_at):
+    def fill(k, spots):
+        for (i, j), planes in open_blocks(in1, k, spots):
             for p in range(2):
                 win[p, j, i * H : (i + 1) * H, :] = planes[p]
 
-    corners = [
-        (0, 0, 7, -1, 0), (0, 256, 6, 1, 1), (2, 0, 9, -1, 2), (2, 256, 8, 1, 3),
-    ]
     forwards = []
-    for k, at, there, side, n in corners:
-        src = in1.at[pl.ds(at_in(k)[0] + at, CORNER)]
-        forwards.append(remote(src, view(in1, there), send1.at[6 + n], recv1.at[there], dev(0, side)))
-    first.down[0].wait_recv()
-    forwards[0].start()
-    forwards[1].start()
-    first.up[0].wait_recv()
-    forwards[2].start()
-    forwards[3].start()
-    fill(0, [(0, 1), (0, 4)], [0, 272], 256)
-    fill(2, [(5, 1), (5, 4)], [0, 272], 256)
+    for n, (k, there, side) in enumerate(((0, 11, -1), (1, 10, 1), (4, 13, -1), (5, 12, 1))):
+        forwards.append(remote(view(in1, k), view(in1, there), send1.at[10 + n], recv1.at[there], dev(0, side)))
+    for n, copy in enumerate((first.down[0], first.down[1], first.up[0], first.up[1])):
+        copy.wait_recv()
+        forwards[n].start()
+    for q in range(2):
+        fill(q, [(0, 1 + COLUMNS[q])])
+        fill(4 + q, [(5, 1 + COLUMNS[q])])
     first.rights.wait_recv()
-    fill(4, [(i, 0) for i in range(1, 5)], [256 * t for t in range(4)], 1024)
+    fill(8, [(i, 0) for i in range(1, 5)])
     first.lefts.wait_recv()
-    fill(5, [(i, 5) for i in range(1, 5)], [256 * t for t in range(4)], 1024)
-    first.down[1].wait_recv()
-    fill(1, [(0, 2), (0, 3)], [0, 256], 512)
-    first.up[1].wait_recv()
-    fill(3, [(5, 2), (5, 3)], [0, 256], 512)
-    for n, (k, spot) in enumerate(((7, (0, 5)), (6, (0, 0)), (9, (5, 5)), (8, (5, 0)))):
+    fill(9, [(i, 5) for i in range(1, 5)])
+    for q in (2, 3):
+        first.down[q].wait_recv()
+        fill(q, [(0, 1 + COLUMNS[q])])
+        first.up[q].wait_recv()
+        fill(4 + q, [(5, 1 + COLUMNS[q])])
+    for n, (k, spot) in enumerate(((11, (0, 5)), (10, (0, 0)), (13, (5, 5)), (12, (5, 0)))):
         forwards[n].wait_recv()
-        fill(k, [spot], [0 if n % 2 == 0 else 16], 256 if n % 2 == 0 else 0)
+        fill(k, [spot])
     for copy in lends:
         copy.start()
     lane = lax.broadcasted_iota(jnp.int32, (FR, H), 1)
@@ -404,12 +401,13 @@
         encode(out2, [at, at + H, at + 256, at + 256 + H], block(0, j) + block(5, j), at + 512)
         there = base + (1 - n) * HALF
         aside.append(
-            remote(out2.at[pl.ds(at, HALF)], in2.at[pl.ds(there, HALF)], send2.at[6 + n], recv2.at[7 - n], dev(0, side))
+            remote(out2.at[pl.ds(at, HALF)], in2.at[pl.ds(there, HALF)], send2.at[10 + n], recv2.at[11 - n], dev(0, side))
         )
         aside[-1].start()
-    put_half(out2, 1, [block(5, 2), block(5, 3)], False)
-    put_half(out2, 3, [block(0, 2), block(0, 3)], False)
-    second.start_second_halves()
+    for q in (3, 2):
+        put_block(out2, q, block(5, 1 + COLUMNS[q]))
+        put_block(out2, 4 + q, block(0, 1 + COLUMNS[q]))
+        second.start(q)
 
     swap.wait()
     half[...] = pg[pl.ds(pl.multiple_of(core * 1024, 1024), 1024), :] + from_core[...]
@@ -429,15 +427,16 @@
         scatter.append(remote(spread.at[there], pieces.at[d], asend.at[1 + d], arecv.at[1 + d], device))
         scatter[-1].start()
 
-    put_strip(out2, 4, [block(i, 0) for i in range(1, 5)])
+    put_strip(out2, 8, [block(i, 0) for i in range(1, 5)])
     second.lefts.start()
-    put_strip(out2, 5, [block(i, 5) for i in range(1, 5)])
+    put_strip(out2, 9, [block(i, 5) for i in range(1, 5)])
     second.rights.start()
     for n, (i, j) in enumerate(((0, 1), (0, 4), (5, 1), (5, 4))):
         planes = block(i, j)
         for p in range(2):
             edge[n, p] = planes[p]
-    second.pass_on()
+    second.pass_on(3)
+    second.pass_on(2)
     for n in range(2):
         aside[n].wait_recv()
     sums = {}
@@ -446,10 +445,10 @@
         scale = tall(scales(in2[at + 512 : at + 528, :]), H)
         for i, off, e in ((0, 0, n), (5, 256, 2 + n)):
             sums[(i, j)] = [edge[e, p] + in2[at + off + p * H : at + off + (p + 1) * H, :].astype(F32) * scale for p in range(2)]
-    put_half(out2, 2, [sums[(0, 1)], sums[(0, 4)]], False)
-    second.up[0].start()
-    put_half(out2, 0, [sums[(5, 1)], sums[(5, 4)]], False)
-    second.down[0].start()
+    for q in (1, 0):
+        put_block(out2, q, sums[(5, 1 + COLUMNS[q])])
+        put_block(out2, 4 + q, sums[(0, 1 + COLUMNS[q])])
+        second.start(q)
 
     def piece_of(ref, k):
         return ref[k, :64, :].astype(F32) * tall(scales(ref[k, 64:, :]), 64)
@@ -479,6 +478,7 @@
             for p in range(2):
                 stage[p, i * H : (i + 1) * H, j * H : (j + 1) * H] = win[p, j + 1, (i + 1) * H : (i + 2) * H, :] - planes[p]
 
+    second.pass_on(1)
     for copy in depth:
         copy.wait()
     total = piece_of(deep_all, 0)
@@ -493,8 +493,8 @@
     cross = [remote(mine, mine, asend.at[38], arecv.at[38], twin)]
     cross[0].start()
 
-    def take(k, spots, first_at, code_at):
-        for (i, j), planes in open_blocks(in2, k, spots, first_at, code_at):
+    def take(k, spots):
+        for (i, j), planes in open_blocks(in2, k, spots):
             for p in range(2):
                 spot = (p, slice(i * H, (i + 1) * H), slice(j * H, (j + 1) * H))
                 stage[spot] = stage[spot] - planes[p]
@@ -506,18 +506,14 @@
         cross[-1].start()
 
     second.rights.wait_recv()
-    take(4, [(i, 0) for i in range(4)], [256 * t for t in range(4)], 1024)
+    take(8, [(i, 0) for i in range(4)])
     second.lefts.wait_recv()
-    take(5, [(i, 3) for i in range(4)], [256 * t for t in range(4)], 1024)
-
-    second.down[1].wait_recv()
-    take(1, [(0, 1), (0, 2)], [0, 256], 512)
-    second.up[1].wait_recv()
-    take(3, [(3, 1), (3, 2)], [0, 256], 512)
-    second.down[0].wait_recv()
-    take(0, [(0, 0), (0, 3)], [0, 256], 512)
-    second.up[0].wait_recv()
-    take(2, [(3, 0), (3, 3)], [0, 256], 512)
+    take(9, [(i, 3) for i in range(4)])
+    for q in (3, 2, 1, 0):
+        second.down[q].wait_recv()
+        take(q, [(0, COLUMNS[q])])
+        second.up[q].wait_recv()
+        take(4 + q, [(3, COLUMNS[q])])
 
     def spell(k, carry):
         value = gathered[k, :64, :].astype(F32) * tall(scales(gathered[k, 64:, :]), 64)
@@ -584,10 +580,10 @@
             pltpu.SMEM((FRAMES,), F32),
             vm((OUT_ROWS, H), I16),
             vm((IN_ROWS, H), I16),
-            vm((2, HALF, H), I16),
+            vm((2, BLOCK, H), I16),
             vm((OUT_ROWS + 2 * HALF, H), I16),
             vm((OUT_ROWS + 2 * HALF, H), I16),
-            vm((2, HALF, H), I16),
+            vm((2, BLOCK, H), I16),
             vm((4, 2, H, H)),
             vm((1024, H)),
             vm((1024, H)),
@@ -596,10 +592,10 @@
             vm((8, PIECE, H), I16),
             vm((32, PIECE, H), I16),
             dma((13,)),
-            dma((12,)),
-            dma((12,)),
-            dma((12,)),
-            dma((12,)),
+            dma((16,)),
+            dma((16,)),
+            dma((16,)),
+            dma((16,)),
             dma((63,)),
             dma((63,)),
         ],

time: 76.7 us -> 73.8 us (0.962)
  Pallas kernels: 73.6 us -> 70.8 us
    pallas_call x1, Pallas kernels: 73.6 us -> 70.8 us  [shards(): pl.pallas_call(kernel, out_shape=(jax.ShapeDtypeStruct(object_field.shape...]
where the time goes in v2:
time: 73.8 us; the launch traced here: 73.7 us
  Pallas kernels  70.8 us (96%)
  local copies, waits for them, and re-layouts  2.29 us (3%)
    pallas_call x1, Pallas kernels, shards(): pl.pallas_call(kernel, out_shape=(jax.ShapeDtypeStruct(object_field.shape...  70.8 us
    unnamed x2, local copies, waits for them, and re-layouts  2.29 us

profile of v2, /device:TPU:1, one launch (start us, length us, event | category | flops | bytes accessed | tf_op | source)
XLA Modules:
  0.0 73.7 jit_solution(4047132563734706251)
XLA Ops:
  0.6 70.8 %step.1 = (f32[2,512,512]{2,1,0:T(8,128)S(1)}, f32[2,2,256,256]{3,2,1,0:T(8,128)S(1)}) custom-call(f32[2,512,512]{2,1,0:T(8,128)} %obj_ref.1, f32[2,2,256,256]{3,2,1,0:T(8,128)} %probe_ref.1, s32[2,4]{1,0:T(2,128)} %bitcast.1, s32[2,2]{1,0:T(2,128)} %lend_pos.1, s32[2]{0:T(128)} %lend_live.1, bf16[4,256,256]{2,1,0:T(8,128)(2,1)} %own_amp.1, ...), custom_call_target="tpu_custom_call" | custom-call | tf_op jit(solution)/shard_map/step/pallas_call | solution.py:560
  71.4 1.3 %copy.14 = f32[2,512,512]{2,1,0:T(8,128)} copy(f32[2,512,512]{2,1,0:T(8,128)S(1)} %get-tuple-element.4) | data formatting | bytes 4194304
  72.7 1.0 %copy.15 = f32[2,2,256,256]{3,2,1,0:T(8,128)} copy(f32[2,2,256,256]{3,2,1,0:T(8,128)S(1)} %get-tuple-element.5) | data formatting | bytes 2097152

commit v3 on v2

--- a/solution.py
+++ b/solution.py
@@ -78,12 +78,6 @@
     return scale_of(-codes.astype(F32))
 
 
-def greet(devices):
-    barrier = pltpu.get_barrier_semaphore()
-    for device in devices:
-        pl.semaphore_signal(barrier, inc=1, device_id=device, device_id_type=MESH)
-
-
 def remote(src, dst, send, recv, device):
     return pltpu.make_async_remote_copy(
         src_ref=src, dst_ref=dst, send_sem=send, recv_sem=recv, device_id=device, device_id_type=MESH
@@ -136,16 +130,33 @@
         there = lax.rem(deep + d, 8)
         high.append((lax.div(there, 2) * 4 + y, x * 4 + lax.rem(there, 2) * 2 + core))
 
-    partners = [dev(*d) for d in ((1, 0), (-1, 0), (0, 1), (0, -1), (2, 0), (-2, 0), (3, 0), (-3, 0), (4, 0), (-4, 0))]
-    partners += [twin] + [f[0] for f in flat] + high
-    greet(partners)
     loads = []
     for p in range(2):
         for j in range(4):
             loads.append((obj_ref.at[p, :, pl.ds(j * H, H)], win.at[p, j + 1, pl.ds(H, TILE), :]))
     loads += [(probe_ref, probe), (own_amp, amp), (perm_ref, perm), (th_ref, th), (tl_ref, tl)]
     loads = [pltpu.make_async_copy(s, d, local.at[k]) for k, (s, d) in enumerate(loads)]
-    for copy in loads:
+    for copy in loads[:8]:
+        copy.start()
+    barrier = pltpu.get_barrier_semaphore()
+
+    def hello(device):
+        pl.semaphore_signal(barrier, inc=1, device_id=device, device_id_type=MESH)
+
+    def first_row():
+        for k in range(1, 5):
+            hello(dev(-k, 0))
+
+    def last_row():
+        for k in range(1, 5):
+            hello(dev(k, 0))
+
+    pl.when(y == 0)(first_row)
+    pl.when(y == 3)(last_row)
+    partners = [dev(0, 1), dev(0, -1)] + [f[0] for f in flat] + high
+    for device in partners:
+        hello(device)
+    for copy in loads[8:]:
         copy.start()
 
     for k in range(OWN):
@@ -177,7 +188,7 @@
         put_block(out1, 4 + q, of_win(0, COLUMNS[q]))
     put_strip(out1, 8, [of_win(i, 0) for i in range(4)])
     put_strip(out1, 9, [of_win(i, 3) for i in range(4)])
-    pl.semaphore_wait(pltpu.get_barrier_semaphore(), len(partners))
+    pl.semaphore_wait(barrier, len(partners) + 2)
 
     class Exchange:
         def __init__(self, out, inn, relay, send, recv):
@@ -372,11 +383,14 @@
 
     lax.fori_loop(0, FRAMES // 2, each, 0)
 
-    def at_rows(ref, index, rows):
-        return ref.at[pl.ds(pl.multiple_of(index * rows, rows), rows)]
-
-    swap = remote(at_rows(pg, 1 - core, 1024), from_core, asend.at[0], arecv.at[0], twin)
-    swap.start()
+    swaps = []
+    for c, dx in enumerate((2, 1, 3, 0)):
+        rows = lax.rem(x + dx, 4) * 256
+        there = pg.at[pl.ds(pl.multiple_of((1 - core) * 1024 + rows, 256), 256)]
+        here = from_core.at[pl.ds(pl.multiple_of(rows, 256), 256)]
+        k = 0 if c == 0 else 62 + c
+        swaps.append(remote(there, here, asend.at[k], arecv.at[k], twin))
+        swaps[-1].start()
 
     spots = [(where[2 * f], lax.div(where[2 * f + 1], H)) for f in range(FRAMES)]
 
@@ -409,23 +423,31 @@
         put_block(out2, 4 + q, block(0, 1 + COLUMNS[q]))
         second.start(q)
 
-    swap.wait()
-    half[...] = pg[pl.ds(pl.multiple_of(core * 1024, 1024), 1024), :] + from_core[...]
-    def spread_out(k, carry):
-        value = half[pl.ds(pl.multiple_of(k * 64, 64), 64), :]
+    def piece_of(ref, k):
+        return ref[k, :64, :].astype(F32) * tall(scales(ref[k, 64:, :]), 64)
+
+    def put_piece(ref, k, value):
         largest = jnp.abs(value[:16])
         for t in range(16, 64, 16):
             largest = jnp.maximum(largest, jnp.abs(value[t : t + 16]))
         code = code_of(largest)
-        spread[k, :64, :] = jnp.round(value * tall(scale_of(code), 64)).astype(jnp.int32).astype(I16)
-        spread[k, 64:, :] = code.astype(jnp.int32).astype(I16)
-        return carry
-
-    lax.fori_loop(0, 16, spread_out, 0)
+        ref[k, :64, :] = jnp.round(value * tall(scale_of(code), 64)).astype(jnp.int32).astype(I16)
+        ref[k, 64:, :] = code.astype(jnp.int32).astype(I16)
+
     scatter = []
-    for d, (device, there, _) in enumerate(flat):
-        scatter.append(remote(spread.at[there], pieces.at[d], asend.at[1 + d], arecv.at[1 + d], device))
-        scatter[-1].start()
+    for c, dx in enumerate((2, 1, 3, 0)):
+        swaps[c].wait_recv()
+        for dy in (2, 1, 3, 0):
+            k = lax.rem(x + dx, 4) * 4 + lax.rem(y + dy, 4)
+            rows = k * 64
+            value = pg[pl.ds(pl.multiple_of(core * 1024 + rows, 64), 64), :] + from_core[pl.ds(pl.multiple_of(rows, 64), 64), :]
+            d = dx * 4 + dy - 1
+            if d < 0:
+                half[...] = value
+                continue
+            put_piece(spread, d, value)
+            scatter.append(remote(spread.at[d], pieces.at[d], asend.at[1 + d], arecv.at[1 + d], flat[d][0]))
+            scatter[-1].start()
 
     put_strip(out2, 8, [block(i, 0) for i in range(1, 5)])
     second.lefts.start()
@@ -450,25 +472,15 @@
         put_block(out2, 4 + q, sums[(0, 1 + COLUMNS[q])])
         second.start(q)
 
-    def piece_of(ref, k):
-        return ref[k, :64, :].astype(F32) * tall(scales(ref[k, 64:, :]), 64)
-
-    def put_piece(ref, k, value):
-        largest = jnp.abs(value[:16])
-        for t in range(16, 64, 16):
-            largest = jnp.maximum(largest, jnp.abs(value[t : t + 16]))
-        code = code_of(largest)
-        ref[k, :64, :] = jnp.round(value * tall(scale_of(code), 64)).astype(jnp.int32).astype(I16)
-        ref[k, 64:, :] = code.astype(jnp.int32).astype(I16)
-
     for copy in scatter:
         copy.wait()
-    total = half[pl.ds(pl.multiple_of(plane * 64, 64), 64), :]
+    total = half[...]
     for d in range(15):
         total = total + piece_of(pieces, d)
     put_piece(deep_all, deep, total)
     depth = []
-    for d, device in enumerate(high):
+    for d in (3, 2, 4, 1, 5, 0, 6):
+        device = high[d]
         depth.append(remote(deep_all.at[deep], deep_all.at[deep], asend.at[16 + d], arecv.at[16 + d], device))
         depth[-1].start()
 
@@ -487,9 +499,11 @@
     put_piece(gathered, core * 16 + plane, total * (1.0 / 1024.0))
     gather = []
     mine = gathered.at[core * 16 + plane]
+    by_hops = sorted(range(15), key=lambda d: -((0, 1, 2, 1)[(d + 1) // 4] + (0, 1, 2, 1)[(d + 1) % 4]))
     for d, (device, _, _) in enumerate(flat):
         gather.append(remote(mine, mine, asend.at[23 + d], arecv.at[23 + d], device))
-        gather[-1].start()
+    for d in by_hops:
+        gather[d].start()
     cross = [remote(mine, mine, asend.at[38], arecv.at[38], twin)]
     cross[0].start()
 
@@ -499,9 +513,9 @@
                 spot = (p, slice(i * H, (i + 1) * H), slice(j * H, (j + 1) * H))
                 stage[spot] = stage[spot] - planes[p]
 
-    for d, (_, _, origin) in enumerate(flat):
+    for d in reversed(by_hops):
         gather[d].wait_recv()
-        part = gathered.at[core * 16 + origin]
+        part = gathered.at[core * 16 + flat[d][2]]
         cross.append(remote(part, part, asend.at[48 + d], arecv.at[48 + d], twin))
         cross[-1].start()
 
@@ -515,19 +529,38 @@
         second.up[q].wait_recv()
         take(4 + q, [(3, COLUMNS[q])])
 
-    def spell(k, carry):
-        value = gathered[k, :64, :].astype(F32) * tall(scales(gathered[k, 64:, :]), 64)
-        m, q, h, part = lax.div(k, 16), lax.rem(lax.div(k, 8), 2), lax.rem(lax.div(k, 4), 2), lax.rem(k, 4)
-        grad_ref[m, q, pl.ds(pl.multiple_of(part * 64, 64), 64), pl.ds(pl.multiple_of(h * H, H), H)] = value
-        return carry
-
+    def spell(own):
+        for k in range(16):
+            value = piece_of(gathered, own * 16 + k)
+            q, h, part = k // 8, k // 4 % 2, k % 4
+            grad_ref[own, q, part * 64 : part * 64 + 64, h * H : (h + 1) * H] = value
+
+    spell(core)
     for copy in cross:
         copy.wait_recv()
-    lax.fori_loop(0, 32, spell, 0)
+    spell(1 - core)
+    for copy in swaps:
+        copy.wait_send()
     first.finish_sends()
     second.finish_sends()
     for copy in forwards + lends + aside + gather + cross:
         copy.wait_send()
+
+
+def write_out(obj_ref, grad_ref, new_ref, out_ref, sems):
+    copies = []
+    for p in range(2):
+        for k in range(2):
+            rows = pl.ds(k * 256, 256)
+            copies.append((obj_ref.at[p, rows], new_ref.at[p, rows]))
+    for m in range(2):
+        for q in range(2):
+            copies.append((grad_ref.at[m, q], out_ref.at[m, q]))
+    copies = [pltpu.make_async_copy(a, b, sems.at[k]) for k, (a, b) in enumerate(copies)]
+    for copy in copies:
+        copy.start()
+    for copy in copies:
+        copy.wait()
 
 
 def tables():
@@ -557,7 +590,7 @@
 
     args = (object_field, probe, own_pos.T, lend_pos, lend_live, own_amp, recv_amp, jnp.asarray(hi), jnp.asarray(lo), jnp.asarray(order))
     held = [pltpu.with_memory_space_constraint(a, pltpu.HBM) for a in args]
-    return pl.pallas_call(
+    new_object, probe_grad = pl.pallas_call(
         kernel,
         out_shape=(
             jax.ShapeDtypeStruct(object_field.shape, F32),
@@ -586,8 +619,8 @@
             vm((2, BLOCK, H), I16),
             vm((4, 2, H, H)),
             vm((1024, H)),
-            vm((1024, H)),
-            vm((16, PIECE, H), I16),
+            vm((64, H)),
+            vm((15, PIECE, H), I16),
             vm((15, PIECE, H), I16),
             vm((8, PIECE, H), I16),
             vm((32, PIECE, H), I16),
@@ -596,12 +629,24 @@
             dma((16,)),
             dma((16,)),
             dma((16,)),
-            dma((63,)),
-            dma((63,)),
+            dma((66,)),
+            dma((66,)),
         ],
         compiler_params=pltpu.CompilerParams(collective_id=0, has_side_effects=True, vmem_limit_bytes=46 << 20),
         name="step",
     )(*held)
+    return pl.pallas_call(
+        write_out,
+        out_shape=(
+            jax.ShapeDtypeStruct(object_field.shape, F32),
+            jax.ShapeDtypeStruct(probe.shape, F32),
+        ),
+        in_specs=[pl.BlockSpec(memory_space=pltpu.VMEM)] * 2,
+        out_specs=(hbm, hbm),
+        scratch_shapes=[dma((8,))],
+        compiler_params=pltpu.CompilerParams(vmem_limit_bytes=8 << 20),
+        name="write_out",
+    )(new_object, probe_grad)
 
 
 def solution(mesh):

time: 73.8 us -> 71.4 us (0.967)
  local copies, waits for them, and re-layouts: 2.29 us -> 0 us
    unnamed x2 -> x0, local copies, waits for them, and re-layouts: 2.29 us -> none
    pallas_call x1, Pallas kernels: 70.8 us -> 68.9 us  [shards(): pl.pallas_call(kernel, out_shape=(jax.ShapeDtypeStruct(object_field.shape...]
    pallas_call x0 -> x1, Pallas kernels: none -> 1.72 us  [shards(): pl.pallas_call(write_out, out_shape=(jax.ShapeDtypeStruct(object_field.sh...]
where the time goes in v3:
time: 71.4 us; the launch traced here: 71.3 us
  Pallas kernels  70.7 us (99%)
    pallas_call x1, Pallas kernels, shards(): pl.pallas_call(kernel, out_shape=(jax.ShapeDtypeStruct(object_field.shape...  68.9 us
    pallas_call x1, Pallas kernels, shards(): pl.pallas_call(write_out, out_shape=(jax.ShapeDtypeStruct(object_field.sh...  1.72 us

profile of v3, /device:TPU:1, one launch (start us, length us, event | category | flops | bytes accessed | tf_op | source)
XLA Modules:
  0.0 71.3 jit_solution(4389285380390497612)
XLA Ops:
  0.6 68.9 %step.1 = (f32[2,512,512]{2,1,0:T(8,128)S(1)}, f32[2,2,256,256]{3,2,1,0:T(8,128)S(1)}) custom-call(f32[2,512,512]{2,1,0:T(8,128)} %obj_ref.1, f32[2,2,256,256]{3,2,1,0:T(8,128)} %probe_ref.1, s32[2,4]{1,0:T(2,128)} %bitcast.1, s32[2,2]{1,0:T(2,128)} %lend_pos.1, s32[2]{0:T(128)} %lend_live.1, bf16[4,256,256]{2,1,0:T(8,128)(2,1)} %own_amp.1, ...), custom_call_target="tpu_custom_call" | custom-call | tf_op jit(solution)/shard_map/step/pallas_call | solution.py:593
  69.6 1.7 %write_out.1 = (f32[2,512,512]{2,1,0:T(8,128)}, f32[2,2,256,256]{3,2,1,0:T(8,128)}) custom-call(f32[2,512,512]{2,1,0:T(8,128)S(1)} %get-tuple-element.4.obj_ref, f32[2,2,256,256]{3,2,1,0:T(8,128)S(1)} %get-tuple-element.5.grad_ref), custom_call_target="tpu_custom_call" | custom-call | tf_op jit(solution)/shard_map/write_out/pallas_call | solution.py:638

commit v4 on v3

--- a/solution.py
+++ b/solution.py
@@ -93,9 +93,13 @@
     return lax.dot_general(a, b, (((1,), (0,)), ((), ())), preferred_element_type=F32)
 
 
-def left(table, x):
+def turned_right(x, table):
     (th, tl), (xh, xl) = table, split(x)
-    return dot(th, xh) + (dot(th, xl) + dot(tl, xh))
+
+    def turned(a, b):
+        return lax.dot_general(a, b, (((0,), (0,)), ((), ())), preferred_element_type=F32)
+
+    return turned(xh, th) + (turned(xl, th) + turned(xh, tl))
 
 
 def right(x, table):
@@ -260,7 +264,7 @@
     inverse = 1.0 / (jnp.full((1, H), jnp.max(power), F32) + 1e-6)
 
     def sort_own(f, carry):
-        amp_sorted[f] = dot(dot(perm[0], amp[f]).astype(BF), perm[1]).astype(BF)
+        amp_sorted[f] = dot(dot(perm[0], amp[f]).astype(BF), perm[1]).T.astype(BF)
         return carry
 
     lax.fori_loop(0, OWN, sort_own, 0)
@@ -333,25 +337,25 @@
                     for q in range(2):
                         whole=jnp.concatenate([cols[u,m,0][:,q*H:(q+1)*H],cols[u,m,1][:,q*H:(q+1)*H]],axis=1)
                         x.append(whole[:H]+whole[H:] if g==0 else whole[:H]-whole[H:])
-                    far[u,m,g]=left(T[g],jnp.concatenate(x,axis=0))
+                    far[u,m,g]=turned_right(jnp.concatenate(x,axis=0),Tt[g])
         B={}
         for u in range(2):
             A=amp_sorted[S[u][0]].astype(F32)
             for g in range(2):
-                power=sum(far[u,m,g][:H]**2+far[u,m,g][H:]**2 for m in range(2))
-                keep=1.0-A[g*H:(g+1)*H]*lax.rsqrt(jnp.maximum(power,1.0))
-                kk=jnp.concatenate([keep,keep],axis=0)
+                power=sum(far[u,m,g][:,:H]**2+far[u,m,g][:,H:]**2 for m in range(2))
+                keep=1.0-A[:,g*H:(g+1)*H]*lax.rsqrt(jnp.maximum(power,1.0))
+                kk=jnp.concatenate([keep,keep],axis=1)
                 for m in range(2):
-                    B[u,m,g]=left(Tt[g],far[u,m,g]*kk)
+                    B[u,m,g]=right(far[u,m,g]*kk,T[g])
         D={}
         for u in range(2):
             for m in range(2):
                 z=[]
                 for q in range(2):
-                    a=B[u,m,0][q*H:(q+1)*H]; b=B[u,m,1][q*H:(q+1)*H]
-                    z.append(jnp.concatenate([a+b,a-b],axis=0))
+                    a=B[u,m,0][:,q*H:(q+1)*H]; b=B[u,m,1][:,q*H:(q+1)*H]
+                    z.append(jnp.concatenate([a+b,a-b],axis=1))
                 for g in range(2):
-                    D[u,m,g]=right(jnp.concatenate([z[0][:,g*H:(g+1)*H],z[1][:,g*H:(g+1)*H]],axis=1),T[g])
+                    D[u,m,g]=turned_right(jnp.concatenate([z[0][g*H:(g+1)*H],z[1][g*H:(g+1)*H]],axis=0),T[g])
         o={}
         for u in range(2):
           for m in range(2):
@@ -376,7 +380,7 @@
         def lent_frames():
             for k in range(2):
                 lends[k].wait_recv()
-                amp_sorted[OWN + k] = dot(dot(perm[0], lent[k]).astype(BF), perm[1]).astype(BF)
+                amp_sorted[OWN + k] = dot(dot(perm[0], lent[k]).astype(BF), perm[1]).T.astype(BF)
 
         pl.when(f == OWN // 2)(lent_frames)
         return two(f, carry)

time: 71.4 us -> 71.1 us (level)
  no operation moved by 1% of the time
where the time goes in v4:
time: 71.1 us
  Pallas kernels  70.4 us (99%)
    pallas_call x1, Pallas kernels, shards(): pl.pallas_call(kernel, out_shape=(jax.ShapeDtypeStruct(object_field.shape...  68.7 us
    pallas_call x1, Pallas kernels, shards(): pl.pallas_call(write_out, out_shape=(jax.ShapeDtypeStruct(object_field.sh...  1.72 us

profile of v4, /device:TPU:1, one launch (start us, length us, event | category | flops | bytes accessed | tf_op | source)
XLA Modules:
  0.0 71.1 jit_solution(91442672787527833)
XLA Ops:
  0.6 68.7 %step.1 = (f32[2,512,512]{2,1,0:T(8,128)S(1)}, f32[2,2,256,256]{3,2,1,0:T(8,128)S(1)}) custom-call(f32[2,512,512]{2,1,0:T(8,128)} %obj_ref.1, f32[2,2,256,256]{3,2,1,0:T(8,128)} %probe_ref.1, s32[2,4]{1,0:T(2,128)} %bitcast.1, s32[2,2]{1,0:T(2,128)} %lend_pos.1, s32[2]{0:T(128)} %lend_live.1, bf16[4,256,256]{2,1,0:T(8,128)(2,1)} %own_amp.1, ...), custom_call_target="tpu_custom_call" | custom-call | tf_op jit(solution)/shard_map/step/pallas_call | solution.py:597
  69.4 1.7 %write_out.1 = (f32[2,512,512]{2,1,0:T(8,128)}, f32[2,2,256,256]{3,2,1,0:T(8,128)}) custom-call(f32[2,512,512]{2,1,0:T(8,128)S(1)} %get-tuple-element.4.obj_ref, f32[2,2,256,256]{3,2,1,0:T(8,128)S(1)} %get-tuple-element.5.grad_ref), custom_call_target="tpu_custom_call" | custom-call | tf_op jit(solution)/shard_map/write_out/pallas_call | solution.py:642
